TPU v7x, 128 devices: a whole 4x4x4 slice. The times are simulated.
128 devices in a mesh: row: 16 (over x, z_lo, core), col: 8 (over y, z_hi).
Axes of the slice: x: 4, y: 4, z: 4 (z_hi: 2, z_lo: 2; z = z_hi * 2 + z_lo), core: 2. Of those that a mesh axis runs over, the one named last changes fastest.
Arguments:
- pair: bfloat16 [512, 512, 128], P('row', 'col'), may hold values from -6 to 6
- pad_mask: int32 [512], replicated, may hold values 0 or 1
- valid_flags: int32 [512], replicated, may hold values 0 or 1
- w_in: bfloat16 [2, 128, 512], replicated, may hold values from -0.5 to 0.5
- w_gate: bfloat16 [2, 128, 128], replicated, may hold values from -0.5 to 0.5
- w_out: bfloat16 [2, 128, 128], replicated, may hold values from -0.5 to 0.5
- gains: float32 [2, 2, 128], replicated, may hold values from 0.1 to 1.9
- shifts: float32 [2, 2, 128], replicated, may hold values from -3 to 3
Outputs:
- result: bfloat16 [512, 512, 128], P('row', 'col')
All inputs are finite; a program needn't handle non-finite values.
Results may differ from a plain program's by a relative error of at most 0.013.
Values may be sent and summed in bfloat16 or wider, within the bound.
A program may use at most 128 MiB of HBM per device.

v0:
```python
import jax
import jax.numpy as jnp
from jax import lax
from jax.sharding import PartitionSpec as P

EPS = 1e-05


def layer_norm(values, gain, shift):
    center = jnp.mean(values, axis=-1, keepdims=True)
    centred = values - center
    variance = jnp.mean(centred * centred, axis=-1, keepdims=True)
    return centred * lax.rsqrt(variance + EPS) * gain + shift


def project_pair(pair, pad_rows, pad_cols, weight_in, weight_gate, gain_pair, shift_pair):
    normed = layer_norm(pair.astype(jnp.float32), gain_pair[0], shift_pair[0]).astype(jnp.bfloat16)
    hidden = weight_in.shape[1] // 4
    flat = normed.reshape(-1, normed.shape[-1])
    projected = jnp.dot(flat, weight_in, preferred_element_type=jnp.float32)
    projected = projected.reshape(normed.shape[0], normed.shape[1], 4 * hidden)
    pair_mask = (pad_rows.astype(jnp.float32)[:, None] * pad_cols.astype(jnp.float32)[None, :])[
        ..., None
    ]
    left_side = (
        jax.nn.sigmoid(projected[..., 2 * hidden : 3 * hidden])
        * projected[..., :hidden]
        * pair_mask
    ).astype(jnp.bfloat16)
    right_side = (
        jax.nn.sigmoid(projected[..., 3 * hidden :])
        * projected[..., hidden : 2 * hidden]
        * pair_mask
    ).astype(jnp.bfloat16)
    gating = jax.nn.sigmoid(jnp.dot(flat, weight_gate, preferred_element_type=jnp.float32)).reshape(
        pair.shape
    )
    return (left_side, right_side, gating)


def finish_pair(pair, mixed, gating, valid_rows, valid_cols, weight_out, gain_pair, shift_pair):
    normed = layer_norm(mixed, gain_pair[1], shift_pair[1]).astype(jnp.bfloat16)
    flat = normed.reshape(-1, normed.shape[-1])
    update = jnp.dot(flat, weight_out, preferred_element_type=jnp.float32).reshape(pair.shape)
    weight = (valid_rows.astype(jnp.float32)[:, None] * valid_cols.astype(jnp.float32)[None, :])[
        ..., None
    ]
    return (pair.astype(jnp.float32) + gating * update * weight).astype(jnp.bfloat16)


def local(pair, pad_mask, valid_flags, w_in, w_gate, w_out, gains, shifts):
    rows_here = pair.shape[0]
    cols_here = pair.shape[1]
    row_index = lax.axis_index("row")
    col_index = lax.axis_index("col")
    row_start = row_index * rows_here
    col_start = col_index * cols_here
    pad_rows = lax.dynamic_slice_in_dim(pad_mask, row_start, rows_here)
    pad_cols = lax.dynamic_slice_in_dim(pad_mask, col_start, cols_here)
    valid_rows = lax.dynamic_slice_in_dim(valid_flags, row_start, rows_here)
    valid_cols = lax.dynamic_slice_in_dim(valid_flags, col_start, cols_here)
    left_side, right_side, gating = project_pair(
        pair, pad_rows, pad_cols, w_in[0], w_gate[0], gains[0], shifts[0]
    )
    right_panel = lax.all_gather(right_side, "row", axis=0, tiled=True)
    chosen = right_panel
    flipped = lax.psum_scatter(
        jnp.einsum("jkh,ikh->jih", chosen, left_side, preferred_element_type=jnp.float32).astype(
            jnp.bfloat16
        ),
        "col",
        scatter_dimension=0,
        tiled=True,
    ).astype(jnp.float32)
    mixed = jnp.transpose(flipped, (1, 0, 2))
    first = finish_pair(pair, mixed, gating, valid_rows, valid_cols, w_out[0], gains[0], shifts[0])
    left_side, right_side, gating = project_pair(
        first, pad_rows, pad_cols, w_in[1], w_gate[1], gains[1], shifts[1]
    )
    left_panel = lax.all_gather(left_side, "col", axis=1, tiled=True)
    chosen = left_panel
    mixed = lax.psum_scatter(
        jnp.einsum("kih,kjh->ijh", chosen, right_side, preferred_element_type=jnp.float32).astype(
            jnp.bfloat16
        ),
        "row",
        scatter_dimension=0,
        tiled=True,
    ).astype(jnp.float32)
    return finish_pair(first, mixed, gating, valid_rows, valid_cols, w_out[1], gains[1], shifts[1])


def solution(mesh):
    placed = (P("row", "col", None), P(), P(), P(), P(), P(), P(), P())
    return jax.shard_map(
        local, mesh=mesh, in_specs=placed, out_specs=P("row", "col", None), check_vma=False
    )
```

profile of v0, /device:TPU:1, one launch (start us, length us, event | category | flops | bytes accessed | tf_op | source)
XLA Modules:
  0.0 417.3 jit_solution(4376899872637227417)
XLA Ops:
  6.5 0.8 dynamic-slice_convert_fusion.3
  7.3 0.8 dynamic-slice_convert_fusion.2
  8.0 1.4 convert_reduce_fusion.1
  9.4 1.7 fusion.20
  11.2 0.1 broadcast_multiply_fusion.1
  11.2 0.8 slice_bitcast_fusion
  12.0 1.6 fusion.23
  13.7 1.6 fusion.62
  15.3 1.4 fusion.39
  16.7 0.0 all-gather.3.cloned.1.call-update
  16.7 0.0 reduce-scatter.3.cloned.1.call-start
  16.7 1.6 copy.45
  18.4 54.3 %all-gather.3.cloned.1.call-done = bf16[512,64,128]{2,1,0:T(8,128)(2,1)} async-done(((bf16[32,64,128]{2,1,0:T(8,128)(2,1)}), bf16[512,64,128]{2,1,0:T(8,128)(2,1)}) %all-gather.3.cloned.1.call-update) | async-done | bytes 8388624 | tf_op jit(solution)/shard_map/all_gather | solution.py:65
  72.6 23.7 %copy.46 = bf16[512,64,128]{1,0,2:T(8,128)(2,1)} copy(bf16[512,64,128]{2,1,0:T(8,128)(2,1)} %all-gather.3.cloned.1.call-done) | data formatting | bytes 16777216 | tf_op jit(solution)/shard_map/all_gather | solution.py:65
  96.4 10.5 %convert_bitcast_fusion.1 = bf16[512,32,128]{0,1,2:T(8,128)(2,1)} fusion(bf16[32,64,128]{1,0,2:T(8,128)(2,1)S(1)} %copy.45, bf16[512,64,128]{1,0,2:T(8,128)(2,1)} %copy.46), kind=kOutput, calls=%fused_computation.1 | convolution fusion | flops 270532608 | bytes 13107200 | tf_op jit(solution)/shard_map/jkh,ikh->jih/dot_general | solution.py:68
  106.8 9.1 %copy.47 = bf16[512,32,128]{2,1,0:T(8,128)(2,1)} copy(bf16[512,32,128]{0,1,2:T(8,128)(2,1)} %convert_bitcast_fusion.1) | data formatting | bytes 8388608 | tf_op jit(solution)/shard_map/convert_element_type | solution.py:68
  116.0 0.0 reduce-scatter.3.cloned.1.call-update
  116.0 0.2 all-gather.5.cloned.1.call-start
  116.2 0.4 copy-done.4
  116.6 0.1 dynamic-slice_convert_fusion.1
  116.7 0.1 dynamic-slice_convert_fusion
  116.8 0.1 broadcast_multiply_fusion
  116.9 0.4 fusion.5
  117.3 82.9 %reduce-scatter.3.cloned.1.call-done = bf16[64,32,128]{2,1,0:T(8,128)(2,1)} async-done(((bf16[512,32,128]{2,1,0:T(8,128)(2,1)}), bf16[64,32,128]{2,1,0:T(8,128)(2,1)}) %reduce-scatter.3.cloned.1.call-update) | async-done | bytes 524304 | tf_op jit(solution)/shard_map/reduce_scatter | solution.py:67
  200.2 1.4 bitcast_reduce_fusion
  201.6 0.1 copy.48
  201.7 0.1 copy.49
  201.7 1.7 fusion.50
  203.4 0.1 copy.50
  203.5 0.1 copy.51
  203.6 1.7 fusion.53
  205.3 0.7 convert_reduce_fusion
  206.0 0.6 fusion.16
  206.7 0.6 fusion.19
  207.3 0.7 fusion.60
  208.0 1.4 fusion.29
  209.4 0.0 all-gather.5.cloned.1.call-update
  209.4 0.0 reduce-scatter.5.cloned.1.call-start
  209.5 1.6 copy.53
  211.1 69.2 %all-gather.5.cloned.1.call-done = bf16[32,512,128]{2,1,0:T(8,128)(2,1)} async-done(((bf16[32,64,128]{2,1,0:T(8,128)(2,1)}), bf16[32,512,128]{2,1,0:T(8,128)(2,1)}) %all-gather.5.cloned.1.call-update) | async-done | bytes 4194320 | tf_op jit(solution)/shard_map/all_gather | solution.py:80
  280.3 7.9 %copy.54 = bf16[32,512,128]{1,0,2:T(8,128)(2,1)} copy(bf16[32,512,128]{2,1,0:T(8,128)(2,1)} %all-gather.5.cloned.1.call-done) | data formatting | bytes 8388608 | tf_op jit(solution)/shard_map/all_gather | solution.py:80
  288.2 7.8 %convert_bitcast_fusion = bf16[512,64,128]{0,1,2:T(8,128)(2,1)} fusion(bf16[32,64,128]{1,0,2:T(8,128)(2,1)S(1)} %copy.53, bf16[32,512,128]{1,0,2:T(8,128)(2,1)} %copy.54), kind=kOutput, calls=%fused_computation | convolution fusion | flops 272629760 | bytes 13107200 | tf_op jit(solution)/shard_map/kih,kjh->ijh/dot_general | solution.py:83
  296.0 13.7 %copy.55 = bf16[512,64,128]{2,1,0:T(8,128)(2,1)} copy(bf16[512,64,128]{0,1,2:T(8,128)(2,1)} %convert_bitcast_fusion) | data formatting | bytes 16777216 | tf_op jit(solution)/shard_map/convert_element_type | solution.py:83
  309.7 0.4 fusion.2
  310.1 94.8 %reduce-scatter.5.cloned.1.call-done = bf16[32,64,128]{2,1,0:T(8,128)(2,1)} async-done(((bf16[512,64,128]{2,1,0:T(8,128)(2,1)}), bf16[32,64,128]{2,1,0:T(8,128)(2,1)}) %reduce-scatter.5.cloned.1.call-update) | async-done | bytes 524304 | tf_op jit(solution)/shard_map/reduce_scatter | solution.py:82
  404.9 1.4 convert_reduce_fusion.2
  406.3 1.7 fusion.24
  408.0 2.7 fusion.9
  (19 shorter events, 0.1 us)
Async XLA Ops:
  6.5 66.1 %all-gather.3.cloned.1.call-start = ((), (), s32[]{:S(2)}) async-start(), calls=%async_computation.2 | async-start | bytes 8912896 | tf_op jit(solution)/shard_map/all_gather | solution.py:65
  16.7 183.5 %reduce-scatter.3.cloned.1.call-start = ((), (), s32[]{:S(2)}) async-start(), calls=%async_computation.3 | async-start | bytes 4718592 | tf_op jit(solution)/shard_map/reduce_scatter | solution.py:67
  116.0 0.7 copy-start.4
  116.0 0.9 copy-start.3
  116.0 89.3 %copy-start = (bf16[32,64,128]{2,1,0:T(8,128)(2,1)S(1)}, bf16[32,64,128]{2,1,0:T(8,128)(2,1)}, u32[]{:S(2)}) copy-start(bf16[32,64,128]{2,1,0:T(8,128)(2,1)} %param.8) | copy-start | bytes 1572868
  116.0 89.3 %copy-start.2 = (bf16[2,128,128]{2,1,0:T(8,128)(2,1)S(1)}, bf16[2,128,128]{2,1,0:T(8,128)(2,1)}, u32[]{:S(2)}) copy-start(bf16[2,128,128]{2,1,0:T(8,128)(2,1)} %param.13) | copy-start | bytes 196612
  116.0 164.3 %all-gather.5.cloned.1.call-start = ((), (), s32[]{:S(2)}) async-start(), calls=%async_computation.4 | async-start | bytes 4718592 | tf_op jit(solution)/shard_map/all_gather | solution.py:80
  117.3 90.0 %copy-start.1 = (bf16[2,128,512]{2,1,0:T(8,128)(2,1)S(1)}, bf16[2,128,512]{2,1,0:T(8,128)(2,1)}, u32[]{:S(2)}) copy-start(bf16[2,128,512]{2,1,0:T(8,128)(2,1)} %param.11) | copy-start | bytes 786436
  209.4 195.5 %reduce-scatter.5.cloned.1.call-start = ((), (), s32[]{:S(2)}) async-start(), calls=%async_computation.5 | async-start | bytes 8912896 | tf_op jit(solution)/shard_map/reduce_scatter | solution.py:82
Sparse Core Ops, SparseCore 0:
  16.8 55.7 all-gather.2
  116.1 84.0 reduce-scatter.2
  209.5 70.7 all-gather.4
  309.8 95.0 reduce-scatter.4
where the time goes:
time: 419 us; the launch traced here: 417 us
  waiting for transfers between devices  301 us (72%)
  local copies, waits for them, and re-layouts  59.2 us (14%)
  matrix products  24.8 us (6%)
  other arithmetic  18.4 us (4%)
  between operations  13.3 us (3%)
    reduce_scatter x1, waiting for transfers between devices, local(): lax.psum_scatter(jnp.einsum('kih,kjh->ijh', chosen, right_side, preferred...  94.8 us
    reduce_scatter x1, waiting for transfers between devices, local(): lax.psum_scatter(jnp.einsum('jkh,ikh->jih', chosen, left_side, preferred_...  82.9 us
    all_gather x1, waiting for transfers between devices, local(): left_panel = lax.all_gather(left_side, 'col', axis=1, tiled=True)  69.2 us
    all_gather x1, waiting for transfers between devices, local(): right_panel = lax.all_gather(right_side, 'row', axis=0, tiled=True)  54.3 us
    all_gather x1, local copies, waits for them, and re-layouts, local(): right_panel = lax.all_gather(right_side, 'row', axis=0, tiled=True)  23.7 us
    convert_element_type x1, local copies, waits for them, and re-layouts, local(): jnp.einsum('kih,kjh->ijh', chosen, right_side, preferred_element_type=jnp...  13.7 us
    dot_general x1, matrix products, local(): jnp.einsum('jkh,ikh->jih', chosen, left_side, preferred_element_type=jnp....  10.5 us
    convert_element_type x1, local copies, waits for them, and re-layouts, local(): jnp.einsum('jkh,ikh->jih', chosen, left_side, preferred_element_type=jnp....  9.13 us
  transfers between devices with their start and end apart: 4, of which 4 were waited for; matrix products, arithmetic and copies ran while one was open for 1% of the time, Pallas kernels for 0%

commit v1 on v0

v1 whole, which is shorter than its diff:
```python
import functools

import jax
import jax.numpy as jnp
from jax import lax
from jax.experimental import pallas as pl
from jax.experimental.pallas import tpu as pltpu
from jax.sharding import PartitionSpec as P

EPS = 1e-05
MESH = pl.DeviceIdType.MESH
F32 = jnp.float32
BF16 = jnp.bfloat16
T = 16
HALF = 64


def sigmoid(v):
    return jax.nn.sigmoid(v)


def kernel(
    nr, nc, pair_ref, pad_s, valid_s, pad_v, valid_v, w_in_ref, w_gate_ref, w_out_ref, gain_ref, shift_ref,
    out_ref,
    send, got, prod, back, wt, gate, first, lay, lay2, big, lhs,
    send_sem, got_sem, back_send_sem, back_sem,
):
    H = nr * nc
    C = pair_ref.shape[-1]
    N = nr * 32
    my_r = lax.axis_index("row")
    my_c = lax.axis_index("col")
    me = my_r * nc + my_c

    def peer(s):
        dr = s // nc
        dc = s % nc
        r = (my_r + dr) % nr
        c = (my_c + dc) % nc
        return r, c

    barrier = pltpu.get_barrier_semaphore()

    def greet(s, carry):
        r, c = peer(s)
        pl.semaphore_signal(barrier, inc=1, device_id=(r, c), device_id_type=MESH)
        return carry

    lax.fori_loop(1, H, greet, 0)

    lane = lax.broadcasted_iota(jnp.int32, (1, 128), 1)
    low = lane < HALF
    sub_low = lax.broadcasted_iota(jnp.int32, (128, 1), 0) < HALF
    odd = my_c % 2

    def col_flags(ref):
        row = ref[pl.ds(my_c // 2, 1), :]
        turned = pltpu.roll(row, HALF, 1)
        lo = jnp.where(odd == 1, turned, row)
        hi = jnp.where(odd == 1, row, turned)
        return jnp.where(low, lo, hi)

    pad_cols = col_flags(pad_v)
    valid_cols = jnp.transpose(jnp.broadcast_to(col_flags(valid_v), (128, 128)))

    def pad_tile(i2):
        top = pad_s[my_r * 32 + i2].astype(F32)
        bottom = pad_s[my_r * 32 + T + i2].astype(F32)
        return jnp.where(low, top, bottom) * pad_cols

    def valid_tile(i2):
        top = valid_s[my_r * 32 + i2].astype(F32)
        bottom = valid_s[my_r * 32 + T + i2].astype(F32)
        return jnp.where(sub_low, top, bottom) * valid_cols

    def project(u, source):
        wt[...] = jnp.transpose(w_in_ref[u].astype(F32)).astype(BF16)
        gain = gain_ref[u, 0:1]
        shift = shift_ref[u, 0:1]
        q = 4

        def chunk(g, carry):
            i2 = g * q
            values = source(i2, q).astype(F32)
            center = jnp.mean(values, axis=-1, keepdims=True)
            centred = values - center
            variance = jnp.mean(centred * centred, axis=-1, keepdims=True)
            normed = (centred * lax.rsqrt(variance + EPS) * gain + shift).astype(BF16)
            gating = sigmoid(jnp.dot(normed, w_gate_ref[u], preferred_element_type=F32))
            gate[pl.ds(i2 * 128, q * 128), :] = gating
            mask = jnp.concatenate([pad_tile(i2 + t) for t in range(q)], axis=1)

            def block(b):
                return lax.dot_general(
                    wt[b * H:(b + 1) * H, :], normed, (((1,), (1,)), ((), ())), preferred_element_type=F32
                )

            left = sigmoid(block(2)) * block(0) * mask
            for t in range(q):
                lay[pl.ds(i2 + t, H, stride=T), :] = left[:, t * 128:(t + 1) * 128]
            right = sigmoid(block(3)) * block(1) * mask
            for t in range(q):
                lay2[pl.ds(i2 + t, H, stride=T), :] = right[:, t * 128:(t + 1) * 128]
            return carry

        lax.fori_loop(0, T // q, chunk, 0)
        hs = 8

        def pack(g, carry):
            a = lay[pl.ds(g * hs * T, hs * T), :].astype(BF16).reshape(hs, T, 128)
            b = lay2[pl.ds(g * hs * T, hs * T), :].astype(BF16).reshape(hs, T, 128)
            send[pl.ds(g * hs, hs), 0] = a
            send[pl.ds(g * hs, hs), 1] = b
            return carry

        lax.fori_loop(0, H // hs, pack, 0)

    def exchange(source, target, s_sem, r_sem):
        own = pltpu.make_async_copy(source.at[me], target.at[me], r_sem)
        own.start()

        def go(s, carry):
            r, c = peer(s)
            pltpu.make_async_remote_copy(
                src_ref=source.at[r * nc + c], dst_ref=target.at[me], send_sem=s_sem, recv_sem=r_sem,
                device_id=(r, c), device_id_type=MESH,
            ).start()
            return carry

        lax.fori_loop(1, H, go, 0)

    def arrive(target, r_sem):
        pltpu.make_async_copy(target, target, r_sem).wait()

    def sent(source, s_sem):
        part = source.at[pl.ds(0, H - 1)]
        pltpu.make_async_copy(part, part, s_sem).wait()

    def halves(tile):
        turned = pltpu.roll(tile, HALF, 1)
        zero = jnp.zeros_like(tile)
        return (
            (jnp.where(low, tile, zero).astype(BF16), jnp.where(low, turned, zero).astype(BF16)),
            (jnp.where(low, zero, turned).astype(BF16), jnp.where(low, zero, tile).astype(BF16)),
        )

    def store_product(u, c0, width, value):
        for c in range(width):
            part = value[:, c * 128:(c + 1) * 128].astype(BF16).reshape(nr, T, 128)
            for r in range(nr):
                prod[u, r * nc + c0 + c] = part[r]

    def outgoing(u):
        box = got.at[u]
        for c in range(nc):
            for r in range(nr):
                lhs[r * T:(r + 1) * T, c * 128:(c + 1) * 128] = box[r * nc + c, 0]

        def build(r, carry):
            for c in range(nc):
                parts = halves(box[r * nc + c, 1].astype(F32))
                for ip in range(2):
                    for jp in range(2):
                        at = (r // 2) * 128 + ip * HALF + (r % 2) * 32 + jp * T
                        big[pl.ds(at, T), c * 128:(c + 1) * 128] = parts[ip][jp]
            return carry

        lax.fori_loop(0, nr, build, 0)
        for c in range(0, nc, 2):
            value = lax.dot_general(
                lhs[...], big[c * 128:(c + 2) * 128, :], (((1,), (1,)), ((), ())), preferred_element_type=F32
            )
            store_product(u, c, 2, value)

    def incoming(u):
        box = got.at[u]
        for c in range(nc):
            block = jnp.concatenate([box[r * nc + c, 0] for r in range(nr)], axis=0)
            turned = jnp.transpose(block.astype(F32)).astype(BF16)
            for kp in range(2):
                for hi in range(2):
                    for ip in range(2):
                        src = ((kp * 2 + hi) * 2 + ip) * T
                        dst = (c * 2 + hi) * T
                        at = (ip * 2 + kp) * nr * T
                        lhs[dst:dst + T, at:at + nr * T] = turned[src:src + T, :]

        def build(r, carry):
            for c in range(nc):
                parts = halves(box[r * nc + c, 1].astype(F32))
                for ip in range(2):
                    for kp in range(2):
                        at = (ip * 2 + kp) * nr * T + r * T
                        big[pl.ds(at, T), c * 128:(c + 1) * 128] = parts[ip][kp]
            return carry

        lax.fori_loop(0, nr, build, 0)
        for c in range(0, nc, 2):
            value = jnp.dot(lhs[...], big[:, c * 128:(c + 2) * 128], preferred_element_type=F32)
            store_product(u, c, 2, value)

    def finish(u, source, emit):
        q = 4
        hs = 8
        box = back.at[u]

        def widen(g, total):
            part = box[pl.ds(g * hs, hs)].astype(F32)
            lay[pl.ds(g * hs * T, hs * T), :] = part.reshape(hs * T, 128)
            return total

        lax.fori_loop(0, H // hs, widen, 0)
        gain = jnp.transpose(jnp.broadcast_to(gain_ref[u, 1:2, :H], (128, H)))
        shift = jnp.transpose(jnp.broadcast_to(shift_ref[u, 1:2, :H], (128, H)))

        def chunk(g, carry):
            i2 = g * q
            for t in range(q):
                mixed = lay[pl.ds(i2 + t, H, stride=T), :]
                center = jnp.mean(mixed, axis=0, keepdims=True)
                centred = mixed - center
                variance = jnp.mean(centred * centred, axis=0, keepdims=True)
                normed = centred * lax.rsqrt(variance + EPS) * gain + shift
                normed = jnp.transpose(normed).astype(BF16)
                update = jnp.dot(normed, w_out_ref[u], preferred_element_type=F32)
                gating = gate[pl.ds((i2 + t) * 128, 128), :]
                value = source(i2 + t, 1).astype(F32) + gating * update * valid_tile(i2 + t)
                emit(i2 + t, value.astype(BF16))
            return carry

        lax.fori_loop(0, T // q, chunk, 0)

    def from_pair(i2, q):
        top = pair_ref[pl.ds(i2, q)]
        bottom = pair_ref[pl.ds(i2 + T, q)]
        return jnp.concatenate([top, bottom], axis=1).reshape(q * 128, C)

    def from_first(i2, q):
        return first[pl.ds(i2, q)].reshape(q * 128, C)

    def to_first(i2, value):
        first[i2] = value

    def to_out(i2, value):
        out_ref[i2] = value[:HALF]
        out_ref[i2 + T] = value[HALF:]

    for u in range(2):
        source = from_pair if u == 0 else from_first
        project(u, source)
        if u == 0:
            pl.semaphore_wait(barrier, H - 1)
        exchange(send, got.at[u], send_sem.at[u], got_sem.at[u])
        arrive(got.at[u], got_sem.at[u])
        if u == 0:
            outgoing(u)
        else:
            incoming(u)
        exchange(prod.at[u], back.at[u], back_send_sem.at[u], back_sem.at[u])
        sent(send, send_sem.at[u])
        arrive(back.at[u], back_sem.at[u])
        finish(u, source, to_first if u == 0 else to_out)
    for u in range(2):
        sent(prod.at[u], back_send_sem.at[u])


def solution(mesh):
    nr, nc = mesh.shape["row"], mesh.shape["col"]

    def local(pair, pad_mask, valid_flags, w_in, w_gate, w_out, gains, shifts):
        H = nr * nc
        C = pair.shape[-1]
        vmem = pl.BlockSpec(memory_space=pltpu.VMEM)
        smem = pl.BlockSpec(memory_space=pltpu.SMEM)
        pad_v = pad_mask.astype(F32).reshape(-1, 128)
        valid_v = valid_flags.astype(F32).reshape(-1, 128)
        return pl.pallas_call(
            functools.partial(kernel, nr, nc),
            out_shape=jax.ShapeDtypeStruct(pair.shape, BF16),
            in_specs=[vmem, smem, smem] + [vmem] * 7,
            out_specs=vmem,
            scratch_shapes=[
                pltpu.VMEM((H, 2, T, 128), BF16),
                pltpu.VMEM((2, H, 2, T, 128), BF16),
                pltpu.VMEM((2, H, T, 128), BF16),
                pltpu.VMEM((2, H, T, 128), BF16),
                pltpu.VMEM((4 * H, C), BF16),
                pltpu.VMEM((T * 128, C), F32),
                pltpu.VMEM((T, 128, C), BF16),
                pltpu.VMEM((H * T, 128), F32),
                pltpu.VMEM((H * T, 128), F32),
                pltpu.VMEM((nc * 128, nc * 128), BF16),
                pltpu.VMEM((nr * T, nc * 128), BF16),
                pltpu.SemaphoreType.DMA((2,)),
                pltpu.SemaphoreType.DMA((2,)),
                pltpu.SemaphoreType.DMA((2,)),
                pltpu.SemaphoreType.DMA((2,)),
            ],
            compiler_params=pltpu.CompilerParams(
                collective_id=0, has_side_effects=True, vmem_limit_bytes=48 * 1024 * 1024
            ),
        )(pair, pad_mask, valid_flags, pad_v, valid_v, w_in, w_gate, w_out, gains, shifts)

    placed = (P("row", "col", None), P(), P(), P(), P(), P(), P(), P())
    return jax.shard_map(
        local, mesh=mesh, in_specs=placed, out_specs=P("row", "col", None), check_vma=False
    )
```

time: 419 us -> 83.8 us (0.20)
  waiting for transfers between devices: 301 us -> 0 us
  Pallas kernels: 0 us -> 77.5 us
  local copies, waits for them, and re-layouts: 59.2 us -> 5.14 us
  matrix products: 24.8 us -> 0 us
  other arithmetic: 18.4 us -> 0.75 us
  between operations: 13.3 us -> 0.03 us
    reduce_scatter x2 -> x0, waiting for transfers between devices: 178 us -> none  [the longest x1 94.8 us: local(): lax.psum_scatter(jnp.einsum('kih,kjh->ijh', chosen, right_side, preferred...]
    all_gather x2 -> x0, waiting for transfers between devices: 124 us -> none  [the longest x1 69.2 us: local(): left_panel = lax.all_gather(left_side, 'col', axis=1, tiled=True)]
    pallas_call x0 -> x1, Pallas kernels: none -> 77.5 us  [local(): pl.pallas_call(functools.partial(kernel, nr, nc), out_shape=jax.ShapeDtyp...]
    all_gather x2 -> x0, local copies, waits for them, and re-layouts: 31.6 us -> none  [the longest x1 23.7 us: local(): right_panel = lax.all_gather(right_side, 'row', axis=0, tiled=True)]
    convert_element_type x4 -> x0, local copies, waits for them, and re-layouts: 26 us -> none  [the longest x1 13.7 us: local(): jnp.einsum('kih,kjh->ijh', chosen, right_side, preferred_element_type=jnp...]
    dot_general x8 -> x0, matrix products: 24.8 us -> none  [the longest x1 10.5 us: local(): jnp.einsum('jkh,ikh->jih', chosen, left_side, preferred_element_type=jnp....]
    reduce_sum x7 -> x0, other arithmetic: 9.85 us -> none  [the longest x4 5.7 us: layer_norm(): variance = jnp.mean(centred * centred, axis=-1, keepdims=True)]
    convert_element_type x9 -> x0, other arithmetic: 8.36 us -> none  [the longest x2 2.26 us: project_pair(): layer_norm(pair.astype(jnp.float32), gain_pair[0], shift_pair[0])]
  transfers between devices with their start and end apart: 4 -> 0, of which waited for: 4 -> 0; matrix products, arithmetic and copies ran while one was open for 1% -> 0% of each run, Pallas kernels for 0% -> 0%
where the time goes in v1:
time: 83.8 us; the launch traced here: 83.5 us
  Pallas kernels  77.5 us (92%)
  local copies, waits for them, and re-layouts  5.14 us (6%)
    pallas_call x1, Pallas kernels, local(): pl.pallas_call(functools.partial(kernel, nr, nc), out_shape=jax.ShapeDtyp...  77.5 us
    unnamed x17, local copies, waits for them, and re-layouts  5.14 us

profile of v1, /device:TPU:1, one launch (start us, length us, event | category | flops | bytes accessed | tf_op | source)
XLA Modules:
  0.0 83.5 jit_solution(10230543583034473554)
XLA Ops:
  0.0 0.0 copy-start.5
  0.0 0.0 copy-start.6
  0.0 0.0 copy-start.7
  0.0 0.8 convert_bitcast_fusion
  0.8 0.0 copy-start.4
  0.8 0.0 copy-done.5
  0.8 0.0 copy-done.6
  0.8 0.0 copy-done.7
  0.8 0.7 copy-done.4
  1.4 0.0 copy-start
  1.4 1.0 %copy-done = bf16[32,64,128]{2,1,0:T(8,128)(2,1)S(1)} copy-done((bf16[32,64,128]{2,1,0:T(8,128)(2,1)S(1)}, bf16[32,64,128]{2,1,0:T(8,128)(2,1)}, u32[]{:S(2)}) %copy-start) | copy-done | bytes 524312
  2.5 0.0 copy-start.1
  2.5 0.9 %copy-done.1 = bf16[2,128,512]{2,1,0:T(8,128)(2,1)S(1)} copy-done((bf16[2,128,512]{2,1,0:T(8,128)(2,1)S(1)}, bf16[2,128,512]{2,1,0:T(8,128)(2,1)}, u32[]{:S(2)}) %copy-start.1) | copy-done | bytes 262168
  3.4 0.0 copy-start.2
  3.4 0.8 %copy-done.2 = bf16[2,128,128]{2,1,0:T(8,128)(2,1)S(1)} copy-done((bf16[2,128,128]{2,1,0:T(8,128)(2,1)S(1)}, bf16[2,128,128]{2,1,0:T(8,128)(2,1)}, u32[]{:S(2)}) %copy-start.2) | copy-done | bytes 65560
  4.3 0.0 copy-start.3
  4.3 0.8 %copy-done.3 = bf16[2,128,128]{2,1,0:T(8,128)(2,1)S(1)} copy-done((bf16[2,128,128]{2,1,0:T(8,128)(2,1)S(1)}, bf16[2,128,128]{2,1,0:T(8,128)(2,1)}, u32[]{:S(2)}) %copy-start.3) | copy-done | bytes 65560
  5.1 77.5 %shard_map.82 = bf16[32,64,128]{2,1,0:T(8,128)(2,1)S(1)} custom-call(bf16[32,64,128]{2,1,0:T(8,128)(2,1)S(1)} %copy-done, s32[512]{0:T(512)S(1)} %copy-done.4, s32[512]{0:T(512)S(1)} %copy-done.5, f32[4,128]{1,0:T(4,128)S(1)} %get-tuple-element.6.pad_v, f32[4,128]{1,0:T(4,128)S(1)} %get-tuple-element.5.valid_v, bf16[2,128,512]{2,1,0:T(8,128)(2,1)S(1)} %copy-done.1, ...), custom_call_target="tpu_custom_call" | custom-call | tf_op jit(solution)/shard_map/pallas_call | solution.py:277
  82.7 0.8 copy.10
Async XLA Ops:
  0.0 0.8 copy-start.5
  0.0 0.8 copy-start.6
  0.0 0.8 copy-start.7
  0.8 0.7 copy-start.4
  1.4 1.0 %copy-start = (bf16[32,64,128]{2,1,0:T(8,128)(2,1)S(1)}, bf16[32,64,128]{2,1,0:T(8,128)(2,1)}, u32[]{:S(2)}) copy-start(bf16[32,64,128]{2,1,0:T(8,128)(2,1)} %pair_ref.1) | copy-start | bytes 1572868
  2.5 0.9 %copy-start.1 = (bf16[2,128,512]{2,1,0:T(8,128)(2,1)S(1)}, bf16[2,128,512]{2,1,0:T(8,128)(2,1)}, u32[]{:S(2)}) copy-start(bf16[2,128,512]{2,1,0:T(8,128)(2,1)} %w_in_ref.1) | copy-start | bytes 786436
  3.4 0.8 %copy-start.2 = (bf16[2,128,128]{2,1,0:T(8,128)(2,1)S(1)}, bf16[2,128,128]{2,1,0:T(8,128)(2,1)}, u32[]{:S(2)}) copy-start(bf16[2,128,128]{2,1,0:T(8,128)(2,1)} %w_gate_ref.1) | copy-start | bytes 196612
  4.3 0.8 %copy-start.3 = (bf16[2,128,128]{2,1,0:T(8,128)(2,1)S(1)}, bf16[2,128,128]{2,1,0:T(8,128)(2,1)}, u32[]{:S(2)}) copy-start(bf16[2,128,128]{2,1,0:T(8,128)(2,1)} %w_out_ref.1) | copy-start | bytes 196612

commit v2 on v1

v2 whole, which is shorter than its diff:
```python
import functools
import itertools

import jax
import jax.numpy as jnp
from jax import lax
from jax.experimental import pallas as pl
from jax.experimental.pallas import tpu as pltpu
from jax.sharding import PartitionSpec as P

EPS = 1e-05
MESH = pl.DeviceIdType.MESH
F32 = jnp.float32
BF16 = jnp.bfloat16
T = 16
HALF = 64
NN = (((1,), (0,)), ((), ()))
NT = (((1,), (1,)), ((), ()))


def sigmoid(v):
    return 0.5 * jnp.tanh(0.5 * v) + 0.5


def dot(a, b, dims=NN):
    return lax.dot_general(a, b, dims, preferred_element_type=F32)


def hops(shift, size):
    return min(shift, size - shift)


def kernel(
    nr, nc, pair_hbm, pad_hbm, valid_hbm, w_in_hbm, w_gate_hbm, w_out_hbm, gain_hbm, shift_hbm,
    out_hbm,
    pair_ref, pad_v, valid_v, w_in_ref, w_gate_ref, w_out_ref, gain_ref, shift_ref, pad_s, valid_s, out_ref,
    send, got, prod, back, wt, nb, gate, first, lay, big, lhs,
    load_sem, send_sem, got_sem, back_send_sem, back_sem, out_sem,
):
    H = nr * nc
    C = pair_ref.shape[-1]
    X, Y = nr // 4, nc // 2
    my_r = lax.axis_index("row")
    my_c = lax.axis_index("col")
    me = my_r * nc + my_c

    xs = [(my_r // 4 + d) % X for d in range(X)]
    ys = [(my_c // 2 + d) % Y for d in range(Y)]
    zs = [((my_c % 2) * 2 + (my_r // 2) % 2 + d) % 4 for d in range(4)]
    ks = [(my_r % 2 + d) % 2 for d in range(2)]
    row_parts = [[xs[dx] * 4 + ks[dk] for dk in range(2)] for dx in range(X)]
    z_lo = [(z % 2) * 2 for z in zs]
    z_hi = [z // 2 for z in zs]

    def peer(shift):
        dx, dy, dz, dk = shift
        return row_parts[dx][dk] + z_lo[dz], ys[dy] * 2 + z_hi[dz]

    def distance(shift):
        dx, dy, dz, dk = shift
        return hops(dx, X) + hops(dy, Y) + hops(dz, 4) + 0.3 * dk

    here = (0, 0, 0, 0)
    shifts = [s for s in itertools.product(range(X), range(Y), range(4), range(2)) if s != here]
    shifts.sort(key=lambda s: -distance(s))

    loads = []
    for i, (a, b) in enumerate((
        (pair_hbm, pair_ref), (w_in_hbm, w_in_ref), (gain_hbm, gain_ref), (shift_hbm, shift_ref), (pad_hbm, pad_v),
        (pad_hbm, pad_s), (w_gate_hbm, w_gate_ref), (w_out_hbm, w_out_ref), (valid_hbm, valid_v),
        (valid_hbm, valid_s),
    )):
        copy = pltpu.make_async_copy(a, b, load_sem.at[i])
        copy.start()
        loads.append(copy)

    barrier = pltpu.get_barrier_semaphore()
    for s in shifts:
        pl.semaphore_signal(barrier, inc=1, device_id=peer(s), device_id_type=MESH)

    lane = lax.broadcasted_iota(jnp.int32, (1, 128), 1)
    low = lane < HALF
    sub_low = lax.broadcasted_iota(jnp.int32, (128, 1), 0) < HALF
    odd = my_c % 2

    def col_flags(ref):
        row = ref[pl.ds(my_c // 2, 1), :].astype(F32)
        turned = pltpu.roll(row, HALF, 1)
        lo = jnp.where(odd == 1, turned, row)
        hi = jnp.where(odd == 1, row, turned)
        return jnp.where(low, lo, hi)

    def flag(ref, i):
        return ref[i // 128, i % 128].astype(F32)

    def pad_tile(cols, i2):
        top = flag(pad_s, my_r * 32 + i2)
        bottom = flag(pad_s, my_r * 32 + T + i2)
        return jnp.where(low, top, bottom) * cols

    def valid_tile(cols, i2):
        top = flag(valid_s, my_r * 32 + i2)
        bottom = flag(valid_s, my_r * 32 + T + i2)
        return jnp.where(sub_low, top, bottom) * cols

    def turn_weights(u):
        wt[u] = jnp.transpose(w_in_ref[u].astype(F32)).astype(BF16)

    q = 4

    def normalize(u, source):
        gain = gain_ref[u, 0:1]
        shift = shift_ref[u, 0:1]

        def chunk(g, carry):
            values = source(g * q, q).astype(F32)
            center = jnp.mean(values, axis=-1, keepdims=True)
            centred = values - center
            variance = jnp.mean(centred * centred, axis=-1, keepdims=True)
            normed = centred * lax.rsqrt(variance + EPS) * gain + shift
            nb[pl.ds(g * q * 128, q * 128), :] = normed.astype(BF16)
            return carry

        lax.fori_loop(0, T // q, chunk, 0)

    def project(u, side):
        cols = col_flags(pad_v)

        def chunk(g, carry):
            normed = nb[pl.ds(g * q * 128, q * 128), :]
            mask = jnp.concatenate([pad_tile(cols, g * q + t) for t in range(q)], axis=1)
            value = dot(wt[u, side * H:(side + 1) * H, :], normed, NT)
            scale = sigmoid(dot(wt[u, (2 + side) * H:(3 + side) * H, :], normed, NT)) * mask
            value = value * scale
            for t in range(q):
                lay[pl.ds(g * q + t, H, stride=T), :] = value[:, t * 128:(t + 1) * 128]
            return carry

        lax.fori_loop(0, T // q, chunk, 0)
        hs = 8

        def pack(g, carry):
            send[u, side, pl.ds(g * hs, hs)] = (
                lay[pl.ds(g * hs * T, hs * T), :].astype(BF16).reshape(hs, T, 128)
            )
            return carry

        lax.fori_loop(0, H // hs, pack, 0)

    def gates(u):
        def chunk(g, carry):
            rows = pl.ds(g * q * 128, q * 128)
            gate[rows, :] = sigmoid(dot(nb[rows, :], w_gate_ref[u]))
            return carry

        lax.fori_loop(0, T // q, chunk, 0)

    def put(source, target, s_sem, r_sem, some):
        for s in some:
            if s == here:
                pltpu.make_async_copy(source.at[me], target.at[me], r_sem).start()
            else:
                r, c = peer(s)
                pltpu.make_async_remote_copy(
                    src_ref=source.at[r * nc + c], dst_ref=target.at[me], send_sem=s_sem, recv_sem=r_sem,
                    device_id=(r, c), device_id_type=MESH,
                ).start()

    def arrive(target, r_sem):
        pltpu.make_async_copy(target, target, r_sem).wait()

    def sent(source, s_sem):
        part = source.at[pl.ds(0, H - 1)]
        pltpu.make_async_copy(part, part, s_sem).wait()

    def halves(tile):
        turned = pltpu.roll(tile, HALF, 1)
        zero = jnp.zeros_like(tile)
        return (
            (jnp.where(low, tile, zero).astype(BF16), jnp.where(low, turned, zero).astype(BF16)),
            (jnp.where(low, zero, turned).astype(BF16), jnp.where(low, zero, tile).astype(BF16)),
        )

    def build(u):
        box = got.at[u, 1]

        def step(r, carry):
            for c in range(nc):
                parts = halves(box[r * nc + c].astype(F32))
                for ip in range(2):
                    for p in range(2):
                        if u == 0:
                            at = (r // 2) * 128 + ip * HALF + (r % 2) * 32 + p * T
                        else:
                            at = (ip * 2 + p) * nr * T + r * T
                        big[pl.ds(pl.multiple_of(at, T), T), c * 128:(c + 1) * 128] = parts[ip][p]
            return carry

        lax.fori_loop(0, nr, step, 0)

    def line_up(u):
        box = got.at[u, 0]
        for c in range(nc):
            if u == 0:
                for r in range(nr):
                    lhs[r * T:(r + 1) * T, c * 128:(c + 1) * 128] = box[r * nc + c]
            else:
                block = jnp.concatenate([box[r * nc + c] for r in range(nr)], axis=0)
                turned = jnp.transpose(block.astype(F32)).astype(BF16)
                for kp, hi, ip in itertools.product(range(2), range(2), range(2)):
                    src = ((kp * 2 + hi) * 2 + ip) * T
                    dst = (c * 2 + hi) * T
                    at = (ip * 2 + kp) * nr * T
                    lhs[dst:dst + T, at:at + nr * T] = turned[src:src + T, :]

    def contract(u):
        for dy in sorted(range(Y), key=lambda d: -hops(d, Y)):
            c0 = ys[dy] * 2
            span = pl.ds(pl.multiple_of(c0 * 128, 256), 256)
            if u == 0:
                value = dot(lhs[...], big[span, :], NT)
            else:
                value = dot(lhs[...], big[:, span])
            for c in range(2):
                part = value[:, c * 128:(c + 1) * 128].astype(BF16).reshape(nr, T, 128)
                for r in range(nr):
                    prod[u, r * nc + c0 + c] = part[r]
            some = [s for s in shifts + [here] if s[1] == dy]
            put(prod.at[u], back.at[u], back_send_sem.at[u], back_sem.at[u], some)

    def finish(u, source, emit):
        hs = 8
        box = back.at[u]

        def widen(g, carry):
            part = box[pl.ds(g * hs, hs)].astype(F32)
            lay[pl.ds(g * hs * T, hs * T), :] = part.reshape(hs * T, 128)
            return carry

        gain = jnp.transpose(jnp.broadcast_to(gain_ref[u, 1:2, :H], (128, H)))
        shift = jnp.transpose(jnp.broadcast_to(shift_ref[u, 1:2, :H], (128, H)))
        cols = jnp.transpose(jnp.broadcast_to(col_flags(valid_v), (128, 128)))
        arrive(box, back_sem.at[u])
        lax.fori_loop(0, H // hs, widen, 0)

        def chunk(g, carry):
            i2 = g * q
            for t in range(q):
                mixed = lay[pl.ds(i2 + t, H, stride=T), :]
                center = jnp.mean(mixed, axis=0, keepdims=True)
                centred = mixed - center
                variance = jnp.mean(centred * centred, axis=0, keepdims=True)
                normed = centred * lax.rsqrt(variance + EPS) * gain + shift
                normed = jnp.transpose(normed).astype(BF16)
                update = dot(normed, w_out_ref[u])
                gating = gate[pl.ds((i2 + t) * 128, 128), :]
                value = source(i2 + t, 1).astype(F32) + gating * update * valid_tile(cols, i2 + t)
                emit(i2 + t, value.astype(BF16))
            return carry

        lax.fori_loop(0, T // q, chunk, 0)

    def from_pair(i2, n):
        top = pair_ref[pl.ds(i2, n)]
        bottom = pair_ref[pl.ds(i2 + T, n)]
        return jnp.concatenate([top, bottom], axis=1).reshape(n * 128, C)

    def from_first(i2, n):
        return first[pl.ds(i2, n)].reshape(n * 128, C)

    def to_first(i2, value):
        first[i2] = value

    def to_out(i2, value):
        out_ref[i2] = value[:HALF]
        out_ref[i2 + T] = value[HALF:]

    for copy in loads[:6]:
        copy.wait()
    turn_weights(0)
    for u in range(2):
        source = from_pair if u == 0 else from_first
        normalize(u, source)
        project(u, 1)
        if u == 0:
            pl.semaphore_wait(barrier, H - 1)
        for side in (1, 0):
            if side == 0:
                project(u, 0)
            put(send.at[u, side], got.at[u, side], send_sem.at[u, side], got_sem.at[u, side], shifts + [here])
        if u == 0:
            for copy in loads[6:]:
                copy.wait()
        gates(u)
        if u == 0:
            turn_weights(1)
        arrive(got.at[u, 1], got_sem.at[u, 1])
        build(u)
        arrive(got.at[u, 0], got_sem.at[u, 0])
        line_up(u)
        contract(u)
        finish(u, source, to_first if u == 0 else to_out)
    last = pltpu.make_async_copy(out_ref, out_hbm, out_sem)
    last.start()
    for u in range(2):
        for side in range(2):
            sent(send.at[u, side], send_sem.at[u, side])
        sent(prod.at[u], back_send_sem.at[u])
    last.wait()


def solution(mesh):
    nr, nc = mesh.shape["row"], mesh.shape["col"]

    def local(pair, pad_mask, valid_flags, w_in, w_gate, w_out, gains, shifts):
        H = nr * nc
        C = pair.shape[-1]
        hbm = pl.BlockSpec(memory_space=pl.ANY)
        pad_mask = pad_mask.reshape(-1, 128)
        valid_flags = valid_flags.reshape(-1, 128)
        operands = (pair, pad_mask, valid_flags, w_in, w_gate, w_out, gains, shifts)
        dma = pltpu.SemaphoreType.DMA
        return pl.pallas_call(
            functools.partial(kernel, nr, nc),
            out_shape=jax.ShapeDtypeStruct(pair.shape, BF16),
            in_specs=[hbm] * len(operands),
            out_specs=hbm,
            scratch_shapes=[pltpu.VMEM(a.shape, a.dtype) for a in operands] + [
                pltpu.SMEM(pad_mask.shape, pad_mask.dtype),
                pltpu.SMEM(valid_flags.shape, valid_flags.dtype),
                pltpu.VMEM(pair.shape, BF16),
                pltpu.VMEM((2, 2, H, T, 128), BF16),
                pltpu.VMEM((2, 2, H, T, 128), BF16),
                pltpu.VMEM((2, H, T, 128), BF16),
                pltpu.VMEM((2, H, T, 128), BF16),
                pltpu.VMEM((2, 4 * H, C), BF16),
                pltpu.VMEM((T * 128, C), BF16),
                pltpu.VMEM((T * 128, C), F32),
                pltpu.VMEM((T, 128, C), BF16),
                pltpu.VMEM((H * T, 128), F32),
                pltpu.VMEM((nc * 128, nc * 128), BF16),
                pltpu.VMEM((nr * T, nc * 128), BF16),
                dma((10,)), dma((2, 2)), dma((2, 2)), dma((2,)), dma((2,)), dma,
            ],
            compiler_params=pltpu.CompilerParams(
                collective_id=0, has_side_effects=True, vmem_limit_bytes=48 * 1024 * 1024
            ),
        )(*operands)

    placed = (P("row", "col", None), P(), P(), P(), P(), P(), P(), P())
    return jax.shard_map(
        local, mesh=mesh, in_specs=placed, out_specs=P("row", "col", None), check_vma=False
    )
```

time: 83.8 us -> 73.2 us (0.87)
  Pallas kernels: 77.5 us -> 65.6 us
  local copies, waits for them, and re-layouts: 5.14 us -> 7.19 us
    pallas_call x1, Pallas kernels: 77.5 us -> 65.6 us  [local(): pl.pallas_call(functools.partial(kernel, nr, nc), out_shape=jax.ShapeDtyp...]
    unnamed x17, local copies, waits for them, and re-layouts: 5.14 us -> 7.19 us
where the time goes in v2:
time: 73.2 us; the launch traced here: 72.8 us
  Pallas kernels  65.6 us (90%)
  local copies, waits for them, and re-layouts  7.19 us (10%)
    pallas_call x1, Pallas kernels, local(): pl.pallas_call(functools.partial(kernel, nr, nc), out_shape=jax.ShapeDtyp...  65.6 us
    unnamed x17, local copies, waits for them, and re-layouts  7.19 us

profile of v2, /device:TPU:1, one launch (start us, length us, event | category | flops | bytes accessed | tf_op | source)
XLA Modules:
  0.0 72.8 jit_solution(4236708371860446049)
XLA Ops:
  0.0 0.0 copy-start.4
  0.0 0.7 copy-done.4
  0.7 0.0 copy-start
  0.7 1.0 %copy-done = bf16[32,64,128]{2,1,0:T(8,128)(2,1)S(1)} copy-done((bf16[32,64,128]{2,1,0:T(8,128)(2,1)S(1)}, bf16[32,64,128]{2,1,0:T(8,128)(2,1)}, u32[]{:S(2)}) %copy-start) | copy-done | bytes 524312
  1.7 0.0 copy-start.1
  1.7 0.9 %copy-done.1 = bf16[2,128,512]{2,1,0:T(8,128)(2,1)S(1)} copy-done((bf16[2,128,512]{2,1,0:T(8,128)(2,1)S(1)}, bf16[2,128,512]{2,1,0:T(8,128)(2,1)}, u32[]{:S(2)}) %copy-start.1) | copy-done | bytes 262168
  2.7 0.0 copy-start.2
  2.7 0.8 %copy-done.2 = bf16[2,128,128]{2,1,0:T(8,128)(2,1)S(1)} copy-done((bf16[2,128,128]{2,1,0:T(8,128)(2,1)S(1)}, bf16[2,128,128]{2,1,0:T(8,128)(2,1)}, u32[]{:S(2)}) %copy-start.2) | copy-done | bytes 65560
  3.5 0.0 copy-start.3
  3.5 0.8 %copy-done.3 = bf16[2,128,128]{2,1,0:T(8,128)(2,1)S(1)} copy-done((bf16[2,128,128]{2,1,0:T(8,128)(2,1)S(1)}, bf16[2,128,128]{2,1,0:T(8,128)(2,1)}, u32[]{:S(2)}) %copy-start.3) | copy-done | bytes 65560
  4.4 0.0 copy-start.5
  4.4 0.7 copy-done.5
  5.0 0.0 copy-start.6
  5.0 0.7 copy-done.6
  5.7 0.0 copy-start.7
  5.7 0.7 copy-done.7
  6.4 65.6 %shard_map.82 = bf16[32,64,128]{2,1,0:T(8,128)(2,1)S(1)} custom-call(bf16[32,64,128]{2,1,0:T(8,128)(2,1)S(1)} %copy-done, s32[4,128]{1,0:T(4,128)S(1)} %bitcast.2, s32[4,128]{1,0:T(4,128)S(1)} %bitcast.3, bf16[2,128,512]{2,1,0:T(8,128)(2,1)S(1)} %copy-done.1, bf16[2,128,128]{2,1,0:T(8,128)(2,1)S(1)} %copy-done.2, bf16[2,128,128]{2,1,0:T(8,128)(2,1)S(1)} %copy-done.3, ...), custom_call_target="tpu_custom_call" | custom-call | tf_op jit(solution)/shard_map/pallas_call | solution.py:323
  72.0 0.8 %copy.10 = bf16[32,64,128]{2,1,0:T(8,128)(2,1)} copy(bf16[32,64,128]{2,1,0:T(8,128)(2,1)S(1)} %shard_map.82) | data formatting | bytes 1048576
Async XLA Ops:
  0.0 0.7 copy-start.4
  0.7 1.0 %copy-start = (bf16[32,64,128]{2,1,0:T(8,128)(2,1)S(1)}, bf16[32,64,128]{2,1,0:T(8,128)(2,1)}, u32[]{:S(2)}) copy-start(bf16[32,64,128]{2,1,0:T(8,128)(2,1)} %pair_hbm.1) | copy-start | bytes 1572868
  1.7 0.9 %copy-start.1 = (bf16[2,128,512]{2,1,0:T(8,128)(2,1)S(1)}, bf16[2,128,512]{2,1,0:T(8,128)(2,1)}, u32[]{:S(2)}) copy-start(bf16[2,128,512]{2,1,0:T(8,128)(2,1)} %w_in_hbm.1) | copy-start | bytes 786436
  2.7 0.8 %copy-start.2 = (bf16[2,128,128]{2,1,0:T(8,128)(2,1)S(1)}, bf16[2,128,128]{2,1,0:T(8,128)(2,1)}, u32[]{:S(2)}) copy-start(bf16[2,128,128]{2,1,0:T(8,128)(2,1)} %w_gate_hbm.1) | copy-start | bytes 196612
  3.5 0.8 %copy-start.3 = (bf16[2,128,128]{2,1,0:T(8,128)(2,1)S(1)}, bf16[2,128,128]{2,1,0:T(8,128)(2,1)}, u32[]{:S(2)}) copy-start(bf16[2,128,128]{2,1,0:T(8,128)(2,1)} %w_out_hbm.1) | copy-start | bytes 196612
  4.4 0.7 copy-start.5
  5.0 0.7 copy-start.6
  5.7 0.7 copy-start.7

commit v3 on v2

v3 whole, which is shorter than its diff:
```python
import functools
import itertools

import jax
import jax.numpy as jnp
from jax import lax
from jax.experimental import pallas as pl
from jax.experimental.pallas import tpu as pltpu
from jax.sharding import PartitionSpec as P

EPS = 1e-05
MESH = pl.DeviceIdType.MESH
F32 = jnp.float32
BF16 = jnp.bfloat16
T = 16
HALF = 64
NN = (((1,), (0,)), ((), ()))
NT = (((1,), (1,)), ((), ()))


def sigmoid(v):
    return 0.5 * jnp.tanh(0.5 * v) + 0.5


def dot(a, b, dims=NN):
    return lax.dot_general(a, b, dims, preferred_element_type=F32)


def hops(shift, size):
    return min(shift, size - shift)


def kernel(
    nr, nc, pair_hbm, pad_hbm, valid_hbm, w_in_hbm, w_gate_hbm, w_out_hbm, gain_hbm, shift_hbm,
    out_hbm,
    pair_ref, pad_v, valid_v, w_in_ref, w_gate_ref, w_out_ref, gain_ref, shift_ref, pad_s, valid_s, out_ref,
    send, got, prod, back, wt, nb, gate, first, lay, lay2, big, lhs,
    load_sem, send_sem, got_sem, back_send_sem, back_sem, out_sem,
):
    H = nr * nc
    C = pair_ref.shape[-1]
    X, Y = nr // 4, nc // 2
    my_r = lax.axis_index("row")
    my_c = lax.axis_index("col")
    me = my_r * nc + my_c

    xs = [(my_r // 4 + d) % X for d in range(X)]
    ys = [(my_c // 2 + d) % Y for d in range(Y)]
    zs = [((my_c % 2) * 2 + (my_r // 2) % 2 + d) % 4 for d in range(4)]
    ks = [(my_r % 2 + d) % 2 for d in range(2)]
    row_parts = [[xs[dx] * 4 + ks[dk] for dk in range(2)] for dx in range(X)]
    z_lo = [(z % 2) * 2 for z in zs]
    z_hi = [z // 2 for z in zs]

    def peer(shift):
        dx, dy, dz, dk = shift
        return row_parts[dx][dk] + z_lo[dz], ys[dy] * 2 + z_hi[dz]

    def distance(shift):
        dx, dy, dz, dk = shift
        return hops(dx, X) + hops(dy, Y) + hops(dz, 4) + 0.3 * dk

    here = (0, 0, 0, 0)
    shifts = [s for s in itertools.product(range(X), range(Y), range(4), range(2)) if s != here]
    shifts.sort(key=lambda s: -distance(s))

    loads = []
    for i, (a, b) in enumerate((
        (pair_hbm, pair_ref), (w_in_hbm, w_in_ref), (gain_hbm, gain_ref), (shift_hbm, shift_ref), (pad_hbm, pad_v),
        (pad_hbm, pad_s), (w_gate_hbm, w_gate_ref), (w_out_hbm, w_out_ref), (valid_hbm, valid_v),
        (valid_hbm, valid_s),
    )):
        copy = pltpu.make_async_copy(a, b, load_sem.at[i])
        copy.start()
        loads.append(copy)

    barrier = pltpu.get_barrier_semaphore()
    for s in shifts:
        pl.semaphore_signal(barrier, inc=1, device_id=peer(s), device_id_type=MESH)

    lane = lax.broadcasted_iota(jnp.int32, (1, 128), 1)
    low = lane < HALF
    sub_low = lax.broadcasted_iota(jnp.int32, (128, 1), 0) < HALF
    odd = my_c % 2

    def col_flags(ref):
        row = ref[pl.ds(my_c // 2, 1), :].astype(F32)
        turned = pltpu.roll(row, HALF, 1)
        lo = jnp.where(odd == 1, turned, row)
        hi = jnp.where(odd == 1, row, turned)
        return jnp.where(low, lo, hi)

    def flag(ref, i):
        return ref[i // 128, i % 128].astype(F32)

    def pad_tile(cols, i2):
        top = flag(pad_s, my_r * 32 + i2)
        bottom = flag(pad_s, my_r * 32 + T + i2)
        return jnp.where(low, top, bottom) * cols

    def valid_tile(cols, i2):
        top = flag(valid_s, my_r * 32 + i2)
        bottom = flag(valid_s, my_r * 32 + T + i2)
        return jnp.where(sub_low, top, bottom) * cols

    def turn_weights(u):
        wt[u] = jnp.transpose(w_in_ref[u].astype(F32)).astype(BF16)

    q = 4
    B = T // 2

    def normalize(u, i2, values):
        values = values.astype(F32)
        center = jnp.mean(values, axis=-1, keepdims=True)
        centred = values - center
        variance = jnp.mean(centred * centred, axis=-1, keepdims=True)
        normed = centred * lax.rsqrt(variance + EPS) * gain_ref[u, 0:1] + shift_ref[u, 0:1]
        normed = normed.astype(BF16)
        nb[pl.ds(i2 * 128, q * 128), :] = normed
        return normed

    def project(u, side, normed, mask, at):
        value = dot(wt[u, side * H:(side + 1) * H, :], normed, NT)
        value = value * (sigmoid(dot(wt[u, (2 + side) * H:(3 + side) * H, :], normed, NT)) * mask)
        for t in range(q):
            lay[pl.ds(at + t, H, stride=T), :] = value[:, t * 128:(t + 1) * 128]

    def pad_mask(cols, i2):
        return jnp.concatenate([pad_tile(cols, i2 + t) for t in range(q)], axis=1)

    def pack(target):
        hs = min(16, H)

        def some(g, carry):
            target[pl.ds(g * hs, hs)] = lay[pl.ds(g * hs * T, hs * T), :].astype(BF16).reshape(hs, T, 128)
            return carry

        for_each(H // hs, some)

    def for_each(n, step):
        if n:
            lax.fori_loop(0, n, step, 0)

    def gates(u):
        def chunk(g, carry):
            rows = pl.ds(g * q * 128, q * 128)
            gate[rows, :] = sigmoid(dot(nb[rows, :], w_gate_ref[u]))
            return carry

        for_each(T // q, chunk)

    def put(source, target, s_sem, r_sem, some):
        for s in some:
            if s == here:
                pltpu.make_async_copy(source.at[me], target.at[me], r_sem).start()
            else:
                r, c = peer(s)
                pltpu.make_async_remote_copy(
                    src_ref=source.at[r * nc + c], dst_ref=target.at[me], send_sem=s_sem, recv_sem=r_sem,
                    device_id=(r, c), device_id_type=MESH,
                ).start()

    def put_block(u, part):
        put(send.at[u, part], got.at[u, part], send_sem.at[u, part], got_sem.at[u, part], shifts + [here])

    def put_back(u, half, some):
        put(prod.at[u, half], back.at[u, half], back_send_sem.at[u, half], back_sem.at[u, half], some)

    def arrive(target, r_sem):
        pltpu.make_async_copy(target, target, r_sem).wait()

    def sent(source, s_sem):
        part = source.at[pl.ds(0, H - 1)]
        pltpu.make_async_copy(part, part, s_sem).wait()

    def halves(tile):
        turned = pltpu.roll(tile, HALF, 1)
        zero = jnp.zeros_like(tile)
        return (
            (jnp.where(low, tile, zero).astype(BF16), jnp.where(low, turned, zero).astype(BF16)),
            (jnp.where(low, zero, turned).astype(BF16), jnp.where(low, zero, tile).astype(BF16)),
        )

    def build_outgoing():
        box = got.at[0, 1]

        def step(r, carry):
            for c in range(nc):
                parts = halves(box[r * nc + c].astype(F32))
                for ip in range(2):
                    for p in range(2):
                        at = (r // 2) * 128 + ip * HALF + (r % 2) * 32 + p * T
                        big[pl.ds(pl.multiple_of(at, T), T), c * 128:(c + 1) * 128] = parts[ip][p]
            return carry

        for_each(nr, step)

    def line_up_outgoing():
        box = got.at[0, 0]
        for c in range(nc):
            for r in range(nr):
                lhs[r * T:(r + 1) * T, c * 128:(c + 1) * 128] = box[r * nc + c]

    def build_incoming(half):
        box = got.at[1, half]

        def step(g, carry):
            r = g * 2
            for c in range(nc):
                tile = jnp.concatenate(
                    [box[r * nc + c].astype(F32)[:B], box[(r + 1) * nc + c].astype(F32)[:B]], axis=0
                )
                parts = halves(tile)
                for ip in range(2):
                    for p in range(2):
                        at = ((ip * 2 + p) * 2 + half) * nr * B + g * T
                        big[pl.ds(pl.multiple_of(at, T), T), c * 128:(c + 1) * 128] = parts[ip][p]
            return carry

        for_each(nr // 2, step)

    def line_up_incoming(half):
        box = got.at[1, half]
        for c in range(nc):
            block = jnp.concatenate([box[r * nc + c].astype(F32)[B:] for r in range(nr)], axis=0)
            turned = jnp.transpose(block).astype(BF16)
            for kp, hi, ip in itertools.product(range(2), range(2), range(2)):
                src = ((kp * 2 + hi) * 2 + ip) * T
                dst = (c * 2 + hi) * T
                at = ((ip * 2 + kp) * 2 + half) * nr * B
                lhs[dst:dst + T, at:at + nr * B] = turned[src:src + T, :]

    def contract(u):
        for dy in sorted(range(Y), key=lambda d: -hops(d, Y)):
            c0 = ys[dy] * 2
            span = pl.ds(pl.multiple_of(c0 * 128, 256), 256)
            if u == 0:
                value = dot(lhs[...], big[span, :], NT)
            else:
                value = dot(lhs[...], big[:, span])
            for c in range(2):
                part = value[:, c * 128:(c + 1) * 128].astype(BF16).reshape(nr, 2, B, 128)
                for r in range(nr):
                    for half in range(2):
                        prod[u, half, r * nc + c0 + c] = part[r, half]
            put_back(u, 0, [s for s in shifts + [here] if s[1] == dy])
        put_back(u, 1, shifts + [here])

    def finish_start(u):
        gain = jnp.transpose(jnp.broadcast_to(gain_ref[u, 1:2, :H], (128, H)))
        shift = jnp.transpose(jnp.broadcast_to(shift_ref[u, 1:2, :H], (128, H)))
        cols = jnp.transpose(jnp.broadcast_to(col_flags(valid_v), (128, 128)))
        return gain, shift, cols

    def widen(u, half):
        hs = min(16, H)
        box = back.at[u, half]
        arrive(box, back_sem.at[u, half])

        def some(g, carry):
            lay2[pl.ds(g * hs * B, hs * B), :] = box[pl.ds(g * hs, hs)].astype(F32).reshape(hs * B, 128)
            return carry

        for_each(H // hs, some)

    def finish(u, half, row, factors, old):
        gain, shift, cols = factors
        i2 = half * B + row
        mixed = lay2[pl.ds(row, H, stride=B), :]
        center = jnp.mean(mixed, axis=0, keepdims=True)
        centred = mixed - center
        variance = jnp.mean(centred * centred, axis=0, keepdims=True)
        normed = centred * lax.rsqrt(variance + EPS) * gain + shift
        normed = jnp.transpose(normed).astype(BF16)
        update = dot(normed, w_out_ref[u])
        gating = gate[pl.ds(i2 * 128, 128), :]
        return (old.astype(F32) + gating * update * valid_tile(cols, i2)).astype(BF16)

    def from_pair(i2, n):
        top = pair_ref[pl.ds(i2, n)]
        bottom = pair_ref[pl.ds(i2 + T, n)]
        return jnp.concatenate([top, bottom], axis=1).reshape(n * 128, C)

    for copy in loads[:6]:
        copy.wait()
    turn_weights(0)
    pad_cols = col_flags(pad_v)

    def right_first(g, carry):
        i2 = g * q
        normed = normalize(0, i2, from_pair(i2, q))
        project(0, 1, normed, pad_mask(pad_cols, i2), i2)
        return carry

    def left_next(g, carry):
        i2 = g * q
        project(0, 0, nb[pl.ds(i2 * 128, q * 128), :], pad_mask(pad_cols, i2), i2)
        return carry

    for_each(T // q, right_first)
    pack(send.at[0, 1])
    pl.semaphore_wait(barrier, H - 1)
    put_block(0, 1)
    for_each(T // q, left_next)
    pack(send.at[0, 0])
    put_block(0, 0)
    for copy in loads[6:]:
        copy.wait()
    gates(0)
    turn_weights(1)
    factors = finish_start(0)
    arrive(got.at[0, 1], got_sem.at[0, 1])
    build_outgoing()
    arrive(got.at[0, 0], got_sem.at[0, 0])
    line_up_outgoing()
    contract(0)

    for half in range(2):
        widen(0, half)

        def middle(g, carry, half=half):
            i2 = half * B + g * q
            values = []
            for t in range(q):
                value = finish(0, half, g * q + t, factors, from_pair(i2 + t, 1))
                first[i2 + t] = value
                values.append(value)
            normed = normalize(1, i2, jnp.concatenate(values, axis=0))
            mask = pad_mask(pad_cols, i2)
            project(1, 1, normed, mask, g * q)
            project(1, 0, normed, mask, B + g * q)
            return carry

        for_each(B // q, middle)
        pack(send.at[1, half])
        put_block(1, half)
    gates(1)
    factors = finish_start(1)
    for half in range(2):
        arrive(got.at[1, half], got_sem.at[1, half])
        build_incoming(half)
        line_up_incoming(half)
    contract(1)
    outs = []
    for half in range(2):
        widen(1, half)

        def end(g, carry, half=half):
            for t in range(q):
                i2 = half * B + g * q + t
                value = finish(1, half, g * q + t, factors, first[i2])
                out_ref[i2] = value[:HALF]
                out_ref[i2 + T] = value[HALF:]
            return carry

        for_each(B // q, end)
        for i, at in enumerate((half * B, T + half * B)):
            rows = pl.ds(at, B)
            copy = pltpu.make_async_copy(out_ref.at[rows], out_hbm.at[rows], out_sem.at[half * 2 + i])
            copy.start()
            outs.append(copy)
    for u in range(2):
        for part in range(2):
            sent(send.at[u, part], send_sem.at[u, part])
            sent(prod.at[u, part], back_send_sem.at[u, part])
    for copy in outs:
        copy.wait()


def solution(mesh):
    nr, nc = mesh.shape["row"], mesh.shape["col"]

    def local(pair, pad_mask, valid_flags, w_in, w_gate, w_out, gains, shifts):
        H = nr * nc
        C = pair.shape[-1]
        hbm = pl.BlockSpec(memory_space=pl.ANY)
        pad_mask = pad_mask.reshape(-1, 128)
        valid_flags = valid_flags.reshape(-1, 128)
        operands = (pair, pad_mask, valid_flags, w_in, w_gate, w_out, gains, shifts)
        dma = pltpu.SemaphoreType.DMA
        return pl.pallas_call(
            functools.partial(kernel, nr, nc),
            out_shape=jax.ShapeDtypeStruct(pair.shape, BF16),
            in_specs=[hbm] * len(operands),
            out_specs=hbm,
            scratch_shapes=[pltpu.VMEM(a.shape, a.dtype) for a in operands] + [
                pltpu.SMEM(pad_mask.shape, pad_mask.dtype),
                pltpu.SMEM(valid_flags.shape, valid_flags.dtype),
                pltpu.VMEM(pair.shape, BF16),
                pltpu.VMEM((2, 2, H, T, 128), BF16),
                pltpu.VMEM((2, 2, H, T, 128), BF16),
                pltpu.VMEM((2, 2, H, T // 2, 128), BF16),
                pltpu.VMEM((2, 2, H, T // 2, 128), BF16),
                pltpu.VMEM((2, 4 * H, C), BF16),
                pltpu.VMEM((T * 128, C), BF16),
                pltpu.VMEM((T * 128, C), F32),
                pltpu.VMEM((T, 128, C), BF16),
                pltpu.VMEM((H * T, 128), F32),
                pltpu.VMEM((H * T // 2, 128), F32),
                pltpu.VMEM((nc * 128, nc * 128), BF16),
                pltpu.VMEM((nr * T, nc * 128), BF16),
                dma((10,)), dma((2, 2)), dma((2, 2)), dma((2, 2)), dma((2, 2)), dma((4,)),
            ],
            compiler_params=pltpu.CompilerParams(
                collective_id=0, has_side_effects=True, vmem_limit_bytes=60 * 1024 * 1024
            ),
        )(*operands)

    placed = (P("row", "col", None), P(), P(), P(), P(), P(), P(), P())
    return jax.shard_map(
        local, mesh=mesh, in_specs=placed, out_specs=P("row", "col", None), check_vma=False
    )
```

time: 73.2 us -> 65.7 us (0.90)
  local copies, waits for them, and re-layouts: 7.19 us -> 1.87 us
  Pallas kernels: 65.6 us -> 63.7 us
    unnamed x17 -> x1, local copies, waits for them, and re-layouts: 7.19 us -> 1.87 us
    pallas_call x1, Pallas kernels: 65.6 us -> 63.7 us  [local(): pl.pallas_call(functools.partial(kernel, nr, nc), out_shape=jax.ShapeDtyp...]
where the time goes in v3:
time: 65.7 us; the launch traced here: 65.5 us
  Pallas kernels  63.7 us (97%)
  local copies, waits for them, and re-layouts  1.87 us (3%)
    pallas_call x1, Pallas kernels, local(): pl.pallas_call(functools.partial(kernel, nr, nc), out_shape=jax.ShapeDtyp...  63.7 us
    unnamed x1, local copies, waits for them, and re-layouts  1.87 us

profile of v3, /device:TPU:1, one launch (start us, length us, event | category | flops | bytes accessed | tf_op | source)
XLA Modules:
  0.0 65.5 jit_solution(4576115158017063806)
XLA Ops:
  0.0 63.7 %shard_map.82 = bf16[32,64,128]{2,1,0:T(8,128)(2,1)} custom-call(bf16[32,64,128]{2,1,0:T(8,128)(2,1)} %pair_hbm.1, s32[4,128]{1,0:T(4,128)} %bitcast.2, s32[4,128]{1,0:T(4,128)} %bitcast.3, bf16[2,128,512]{2,1,0:T(8,128)(2,1)} %w_in_hbm.1, bf16[2,128,128]{2,1,0:T(8,128)(2,1)} %w_gate_hbm.1, bf16[2,128,128]{2,1,0:T(8,128)(2,1)} %w_out_hbm.1, ...), custom_call_target="tpu_custom_call" | custom-call | tf_op jit(solution)/shard_map/pallas_call | solution.py:381
  63.7 1.9 %copy.10 = bf16[32,64,128]{2,1,0:T(8,128)(2,1)} copy(bf16[32,64,128]{2,1,0:T(8,128)(2,1)} %shard_map.82) | data formatting | bytes 1048576

commit v4 on v3

--- a/solution.py
+++ b/solution.py
@@ -34,8 +34,8 @@
     nr, nc, pair_hbm, pad_hbm, valid_hbm, w_in_hbm, w_gate_hbm, w_out_hbm, gain_hbm, shift_hbm,
     out_hbm,
     pair_ref, pad_v, valid_v, w_in_ref, w_gate_ref, w_out_ref, gain_ref, shift_ref, pad_s, valid_s, out_ref,
-    send, got, prod, back, wt, nb, gate, first, lay, lay2, big, lhs,
-    load_sem, send_sem, got_sem, back_send_sem, back_sem, out_sem,
+    send, got, send_left, got_left, prod, back, wt, wg, wo, nb, gate, held, lay, lay2, big, lhs,
+    load_sem, send_sem, got_sem, left_send_sem, left_sem, back_send_sem, back_sem, out_sem,
 ):
     H = nr * nc
     C = pair_ref.shape[-1]
@@ -80,7 +80,6 @@
 
     lane = lax.broadcasted_iota(jnp.int32, (1, 128), 1)
     low = lane < HALF
-    sub_low = lax.broadcasted_iota(jnp.int32, (128, 1), 0) < HALF
     odd = my_c % 2
 
     def col_flags(ref):
@@ -93,46 +92,50 @@
     def flag(ref, i):
         return ref[i // 128, i % 128].astype(F32)
 
-    def pad_tile(cols, i2):
-        top = flag(pad_s, my_r * 32 + i2)
-        bottom = flag(pad_s, my_r * 32 + T + i2)
-        return jnp.where(low, top, bottom) * cols
-
-    def valid_tile(cols, i2):
-        top = flag(valid_s, my_r * 32 + i2)
-        bottom = flag(valid_s, my_r * 32 + T + i2)
-        return jnp.where(sub_low, top, bottom) * cols
-
-    def turn_weights(u):
-        wt[u] = jnp.transpose(w_in_ref[u].astype(F32)).astype(BF16)
-
     q = 4
     B = T // 2
 
-    def normalize(u, i2, values):
-        values = values.astype(F32)
-        center = jnp.mean(values, axis=-1, keepdims=True)
+    def flags(ref, cols, i2):
+        tiles = []
+        for t in range(q):
+            top = flag(ref, my_r * 32 + i2 + t)
+            bottom = flag(ref, my_r * 32 + T + i2 + t)
+            tiles.append(jnp.where(low, top, bottom) * cols)
+        return jnp.concatenate(tiles, axis=1)
+
+    def turn(value):
+        return jnp.transpose(value.astype(F32))
+
+    def turn_weights(u):
+        turned = turn(w_in_ref[u]).astype(BF16)
+        for i, block in enumerate((0, 2, 1, 3)):
+            wt[u, i * H:(i + 1) * H] = turned[block * H:(block + 1) * H]
+
+    def turn_small(u):
+        wg[u] = turn(w_gate_ref[u]).astype(BF16)
+        wo[u] = turn(w_out_ref[u]).astype(BF16)
+
+    def column(ref, u, which, n):
+        return jnp.transpose(jnp.broadcast_to(ref[u, which:which + 1, :n], (128, n)))
+
+    def norm(values, gain, shift):
+        center = jnp.mean(values, axis=0, keepdims=True)
         centred = values - center
-        variance = jnp.mean(centred * centred, axis=-1, keepdims=True)
-        normed = centred * lax.rsqrt(variance + EPS) * gain_ref[u, 0:1] + shift_ref[u, 0:1]
-        normed = normed.astype(BF16)
-        nb[pl.ds(i2 * 128, q * 128), :] = normed
-        return normed
-
-    def project(u, side, normed, mask, at):
-        value = dot(wt[u, side * H:(side + 1) * H, :], normed, NT)
-        value = value * (sigmoid(dot(wt[u, (2 + side) * H:(3 + side) * H, :], normed, NT)) * mask)
+        variance = jnp.mean(centred * centred, axis=0, keepdims=True)
+        return (centred * lax.rsqrt(variance + EPS) * gain + shift).astype(BF16)
+
+    def project(u, side, normed, mask, at, stride):
+        both = dot(wt[u, side * 2 * H:(side + 1) * 2 * H, :], normed)
+        value = both[:H] * (sigmoid(both[H:]) * mask)
         for t in range(q):
-            lay[pl.ds(at + t, H, stride=T), :] = value[:, t * 128:(t + 1) * 128]
-
-    def pad_mask(cols, i2):
-        return jnp.concatenate([pad_tile(cols, i2 + t) for t in range(q)], axis=1)
-
-    def pack(target):
+            lay[pl.ds(at + t, H, stride=stride), :] = value[:, t * 128:(t + 1) * 128]
+
+    def pack(target, rows):
         hs = min(16, H)
 
         def some(g, carry):
-            target[pl.ds(g * hs, hs)] = lay[pl.ds(g * hs * T, hs * T), :].astype(BF16).reshape(hs, T, 128)
+            part = lay[pl.ds(g * hs * rows, hs * rows), :].astype(BF16)
+            target[pl.ds(g * hs, hs)] = part.reshape(hs, rows, 128)
             return carry
 
         for_each(H // hs, some)
@@ -143,8 +146,7 @@
 
     def gates(u):
         def chunk(g, carry):
-            rows = pl.ds(g * q * 128, q * 128)
-            gate[rows, :] = sigmoid(dot(nb[rows, :], w_gate_ref[u]))
+            gate[g] = sigmoid(dot(wg[u], nb[g]))
             return carry
 
         for_each(T // q, chunk)
@@ -160,8 +162,11 @@
                     device_id=(r, c), device_id_type=MESH,
                 ).start()
 
-    def put_block(u, part):
-        put(send.at[u, part], got.at[u, part], send_sem.at[u, part], got_sem.at[u, part], shifts + [here])
+    def put_block(i):
+        put(send.at[i], got.at[i], send_sem.at[i], got_sem.at[i], shifts + [here])
+
+    def put_left(half):
+        put(send_left.at[half], got_left.at[half], left_send_sem.at[half], left_sem.at[half], shifts + [here])
 
     def put_back(u, half, some):
         put(prod.at[u, half], back.at[u, half], back_send_sem.at[u, half], back_sem.at[u, half], some)
@@ -182,7 +187,7 @@
         )
 
     def build_outgoing():
-        box = got.at[0, 1]
+        box = got.at[0]
 
         def step(r, carry):
             for c in range(nc):
@@ -195,14 +200,16 @@
 
         for_each(nr, step)
 
-    def line_up_outgoing():
-        box = got.at[0, 0]
+    def line_up_outgoing(half):
+        box = got_left.at[half]
         for c in range(nc):
-            for r in range(nr):
-                lhs[r * T:(r + 1) * T, c * 128:(c + 1) * 128] = box[r * nc + c]
+            for r in range(0, nr, 2):
+                pair = jnp.concatenate([box[r * nc + c].astype(F32), box[(r + 1) * nc + c].astype(F32)], axis=0)
+                at = half * nr * B + r * B
+                lhs[at:at + T, c * 128:(c + 1) * 128] = pair.astype(BF16)
 
     def build_incoming(half):
-        box = got.at[1, half]
+        box = got.at[1 + half]
 
         def step(g, carry):
             r = g * 2
@@ -220,7 +227,7 @@
         for_each(nr // 2, step)
 
     def line_up_incoming(half):
-        box = got.at[1, half]
+        box = got.at[1 + half]
         for c in range(nc):
             block = jnp.concatenate([box[r * nc + c].astype(F32)[B:] for r in range(nr)], axis=0)
             turned = jnp.transpose(block).astype(BF16)
@@ -230,27 +237,31 @@
                 at = ((ip * 2 + kp) * 2 + half) * nr * B
                 lhs[dst:dst + T, at:at + nr * B] = turned[src:src + T, :]
 
-    def contract(u):
-        for dy in sorted(range(Y), key=lambda d: -hops(d, Y)):
+    columns = sorted(range(Y), key=lambda d: -hops(d, Y))
+
+    def contract_outgoing(half):
+        for dy in columns:
             c0 = ys[dy] * 2
             span = pl.ds(pl.multiple_of(c0 * 128, 256), 256)
-            if u == 0:
-                value = dot(lhs[...], big[span, :], NT)
-            else:
-                value = dot(lhs[...], big[:, span])
+            value = dot(lhs[half * nr * B:(half + 1) * nr * B, :], big[span, :], NT)
+            for c in range(2):
+                part = value[:, c * 128:(c + 1) * 128].astype(BF16).reshape(nr, B, 128)
+                for r in range(nr):
+                    prod[0, half, r * nc + c0 + c] = part[r]
+            put_back(0, half, [s for s in shifts + [here] if s[1] == dy])
+
+    def contract_incoming():
+        for dy in columns:
+            c0 = ys[dy] * 2
+            span = pl.ds(pl.multiple_of(c0 * 128, 256), 256)
+            value = dot(lhs[...], big[:, span])
             for c in range(2):
                 part = value[:, c * 128:(c + 1) * 128].astype(BF16).reshape(nr, 2, B, 128)
                 for r in range(nr):
                     for half in range(2):
-                        prod[u, half, r * nc + c0 + c] = part[r, half]
-            put_back(u, 0, [s for s in shifts + [here] if s[1] == dy])
-        put_back(u, 1, shifts + [here])
-
-    def finish_start(u):
-        gain = jnp.transpose(jnp.broadcast_to(gain_ref[u, 1:2, :H], (128, H)))
-        shift = jnp.transpose(jnp.broadcast_to(shift_ref[u, 1:2, :H], (128, H)))
-        cols = jnp.transpose(jnp.broadcast_to(col_flags(valid_v), (128, 128)))
-        return gain, shift, cols
+                        prod[1, half, r * nc + c0 + c] = part[r, half]
+            put_back(1, 0, [s for s in shifts + [here] if s[1] == dy])
+        put_back(1, 1, shifts + [here])
 
     def widen(u, half):
         hs = min(16, H)
@@ -263,18 +274,13 @@
 
         for_each(H // hs, some)
 
-    def finish(u, half, row, factors, old):
-        gain, shift, cols = factors
+    def finish(u, half, row, factors):
+        gain, shift = factors
         i2 = half * B + row
-        mixed = lay2[pl.ds(row, H, stride=B), :]
-        center = jnp.mean(mixed, axis=0, keepdims=True)
-        centred = mixed - center
-        variance = jnp.mean(centred * centred, axis=0, keepdims=True)
-        normed = centred * lax.rsqrt(variance + EPS) * gain + shift
-        normed = jnp.transpose(normed).astype(BF16)
-        update = dot(normed, w_out_ref[u])
-        gating = gate[pl.ds(i2 * 128, 128), :]
-        return (old.astype(F32) + gating * update * valid_tile(cols, i2)).astype(BF16)
+        normed = [norm(lay2[pl.ds(row + t, H, stride=B), :], gain, shift) for t in range(q)]
+        update = dot(wo[u], jnp.concatenate(normed, axis=1))
+        old = jnp.concatenate([held[i2 + t].astype(F32) for t in range(q)], axis=1)
+        return old + gate[i2 // q] * update * flags(valid_s, valid_cols, i2)
 
     def from_pair(i2, n):
         top = pair_ref[pl.ds(i2, n)]
@@ -285,70 +291,87 @@
         copy.wait()
     turn_weights(0)
     pad_cols = col_flags(pad_v)
+    gain, shift = column(gain_ref, 0, 0, C), column(shift_ref, 0, 0, C)
 
     def right_first(g, carry):
         i2 = g * q
-        normed = normalize(0, i2, from_pair(i2, q))
-        project(0, 1, normed, pad_mask(pad_cols, i2), i2)
+        values = turn(from_pair(i2, q))
+        normed = []
+        for t in range(q):
+            tile = values[:, t * 128:(t + 1) * 128]
+            held[i2 + t] = tile.astype(BF16)
+            normed.append(norm(tile, gain, shift))
+        normed = jnp.concatenate(normed, axis=1)
+        nb[g] = normed
+        project(0, 1, normed, flags(pad_s, pad_cols, i2), i2, T)
         return carry
 
-    def left_next(g, carry):
-        i2 = g * q
-        project(0, 0, nb[pl.ds(i2 * 128, q * 128), :], pad_mask(pad_cols, i2), i2)
-        return carry
-
     for_each(T // q, right_first)
-    pack(send.at[0, 1])
+    pack(send.at[0], T)
     pl.semaphore_wait(barrier, H - 1)
-    put_block(0, 1)
-    for_each(T // q, left_next)
-    pack(send.at[0, 0])
-    put_block(0, 0)
+    put_block(0)
+    for half in range(2):
+        def left_next(g, carry, half=half):
+            i2 = half * B + g * q
+            project(0, 0, nb[half * (B // q) + g], flags(pad_s, pad_cols, i2), g * q, B)
+            return carry
+
+        for_each(B // q, left_next)
+        pack(send_left.at[half], B)
+        put_left(half)
     for copy in loads[6:]:
         copy.wait()
+    valid_cols = col_flags(valid_v)
+    turn_small(0)
     gates(0)
     turn_weights(1)
-    factors = finish_start(0)
-    arrive(got.at[0, 1], got_sem.at[0, 1])
+    turn_small(1)
+    factors = column(gain_ref, 0, 1, H), column(shift_ref, 0, 1, H)
+    gain1, shift1 = column(gain_ref, 1, 0, C), column(shift_ref, 1, 0, C)
+    arrive(got.at[0], got_sem.at[0])
     build_outgoing()
-    arrive(got.at[0, 0], got_sem.at[0, 0])
-    line_up_outgoing()
-    contract(0)
+    for half in range(2):
+        arrive(got_left.at[half], left_sem.at[half])
+        line_up_outgoing(half)
+        contract_outgoing(half)
 
     for half in range(2):
         widen(0, half)
 
         def middle(g, carry, half=half):
             i2 = half * B + g * q
-            values = []
+            values = finish(0, half, g * q, factors).astype(BF16)
+            normed = []
             for t in range(q):
-                value = finish(0, half, g * q + t, factors, from_pair(i2 + t, 1))
-                first[i2 + t] = value
-                values.append(value)
-            normed = normalize(1, i2, jnp.concatenate(values, axis=0))
-            mask = pad_mask(pad_cols, i2)
-            project(1, 1, normed, mask, g * q)
-            project(1, 0, normed, mask, B + g * q)
+                tile = values[:, t * 128:(t + 1) * 128]
+                held[i2 + t] = tile
+                normed.append(norm(tile.astype(F32), gain1, shift1))
+            normed = jnp.concatenate(normed, axis=1)
+            nb[half * (B // q) + g] = normed
+            mask = flags(pad_s, pad_cols, i2)
+            project(1, 1, normed, mask, g * q, T)
+            project(1, 0, normed, mask, B + g * q, T)
             return carry
 
         for_each(B // q, middle)
-        pack(send.at[1, half])
-        put_block(1, half)
+        pack(send.at[1 + half], T)
+        put_block(1 + half)
     gates(1)
-    factors = finish_start(1)
-    for half in range(2):
-        arrive(got.at[1, half], got_sem.at[1, half])
+    factors = column(gain_ref, 1, 1, H), column(shift_ref, 1, 1, H)
+    for half in range(2):
+        arrive(got.at[1 + half], got_sem.at[1 + half])
         build_incoming(half)
         line_up_incoming(half)
-    contract(1)
+    contract_incoming()
     outs = []
     for half in range(2):
         widen(1, half)
 
         def end(g, carry, half=half):
+            values = finish(1, half, g * q, factors)
             for t in range(q):
                 i2 = half * B + g * q + t
-                value = finish(1, half, g * q + t, factors, first[i2])
+                value = jnp.transpose(values[:, t * 128:(t + 1) * 128]).astype(BF16)
                 out_ref[i2] = value[:HALF]
                 out_ref[i2 + T] = value[HALF:]
             return carry
@@ -359,10 +382,12 @@
             copy = pltpu.make_async_copy(out_ref.at[rows], out_hbm.at[rows], out_sem.at[half * 2 + i])
             copy.start()
             outs.append(copy)
-    for u in range(2):
-        for part in range(2):
-            sent(send.at[u, part], send_sem.at[u, part])
-            sent(prod.at[u, part], back_send_sem.at[u, part])
+    for i in range(3):
+        sent(send.at[i], send_sem.at[i])
+    for half in range(2):
+        sent(send_left.at[half], left_send_sem.at[half])
+        for u in range(2):
+            sent(prod.at[u, half], back_send_sem.at[u, half])
     for copy in outs:
         copy.wait()
 
@@ -387,19 +412,23 @@
                 pltpu.SMEM(pad_mask.shape, pad_mask.dtype),
                 pltpu.SMEM(valid_flags.shape, valid_flags.dtype),
                 pltpu.VMEM(pair.shape, BF16),
-                pltpu.VMEM((2, 2, H, T, 128), BF16),
-                pltpu.VMEM((2, 2, H, T, 128), BF16),
+                pltpu.VMEM((3, H, T, 128), BF16),
+                pltpu.VMEM((3, H, T, 128), BF16),
+                pltpu.VMEM((2, H, T // 2, 128), BF16),
+                pltpu.VMEM((2, H, T // 2, 128), BF16),
                 pltpu.VMEM((2, 2, H, T // 2, 128), BF16),
                 pltpu.VMEM((2, 2, H, T // 2, 128), BF16),
                 pltpu.VMEM((2, 4 * H, C), BF16),
-                pltpu.VMEM((T * 128, C), BF16),
-                pltpu.VMEM((T * 128, C), F32),
-                pltpu.VMEM((T, 128, C), BF16),
+                pltpu.VMEM((2, C, C), BF16),
+                pltpu.VMEM((2, C, H), BF16),
+                pltpu.VMEM((T // 4, C, 512), BF16),
+                pltpu.VMEM((T // 4, C, 512), F32),
+                pltpu.VMEM((T, C, 128), BF16),
                 pltpu.VMEM((H * T, 128), F32),
                 pltpu.VMEM((H * T // 2, 128), F32),
                 pltpu.VMEM((nc * 128, nc * 128), BF16),
                 pltpu.VMEM((nr * T, nc * 128), BF16),
-                dma((10,)), dma((2, 2)), dma((2, 2)), dma((2, 2)), dma((2, 2)), dma((4,)),
+                dma((10,)), dma((3,)), dma((3,)), dma((2,)), dma((2,)), dma((2, 2)), dma((2, 2)), dma((4,)),
             ],
             compiler_params=pltpu.CompilerParams(
                 collective_id=0, has_side_effects=True, vmem_limit_bytes=60 * 1024 * 1024

time: 65.7 us -> 64.3 us (0.979)
  Pallas kernels: 63.7 us -> 62.2 us
    pallas_call x1, Pallas kernels: 63.7 us -> 62.2 us  [local(): pl.pallas_call(functools.partial(kernel, nr, nc), out_shape=jax.ShapeDtyp...]
where the time goes in v4:
time: 64.3 us; the launch traced here: 64.1 us
  Pallas kernels  62.2 us (97%)
  local copies, waits for them, and re-layouts  1.87 us (3%)
    pallas_call x1, Pallas kernels, local(): pl.pallas_call(functools.partial(kernel, nr, nc), out_shape=jax.ShapeDtyp...  62.2 us
    unnamed x1, local copies, waits for them, and re-layouts  1.87 us

profile of v4, /device:TPU:1, one launch (start us, length us, event | category | flops | bytes accessed | tf_op | source)
XLA Modules:
  0.0 64.1 jit_solution(2497227439790631653)
XLA Ops:
  0.0 62.2 %shard_map.82 = bf16[32,64,128]{2,1,0:T(8,128)(2,1)} custom-call(bf16[32,64,128]{2,1,0:T(8,128)(2,1)} %pair_hbm.1, s32[4,128]{1,0:T(4,128)} %bitcast.2, s32[4,128]{1,0:T(4,128)} %bitcast.3, bf16[2,128,512]{2,1,0:T(8,128)(2,1)} %w_in_hbm.1, bf16[2,128,128]{2,1,0:T(8,128)(2,1)} %w_gate_hbm.1, bf16[2,128,128]{2,1,0:T(8,128)(2,1)} %w_out_hbm.1, ...), custom_call_target="tpu_custom_call" | custom-call | tf_op jit(solution)/shard_map/pallas_call | solution.py:406
  62.2 1.9 %copy.10 = bf16[32,64,128]{2,1,0:T(8,128)(2,1)} copy(bf16[32,64,128]{2,1,0:T(8,128)(2,1)} %shard_map.82) | data formatting | bytes 1048576

commit v5 on v4

--- a/solution.py
+++ b/solution.py
@@ -62,7 +62,7 @@
 
     here = (0, 0, 0, 0)
     shifts = [s for s in itertools.product(range(X), range(Y), range(4), range(2)) if s != here]
-    shifts.sort(key=lambda s: -distance(s))
+    shifts.sort(key=lambda s: (-distance(s), (s[0] * 37 + s[1] * 53 + s[2] * 71 + s[3] * 19) % 29))
 
     loads = []
     for i, (a, b) in enumerate((
@@ -248,7 +248,7 @@
                 part = value[:, c * 128:(c + 1) * 128].astype(BF16).reshape(nr, B, 128)
                 for r in range(nr):
                     prod[0, half, r * nc + c0 + c] = part[r]
-            put_back(0, half, [s for s in shifts + [here] if s[1] == dy])
+        put_back(0, half, shifts + [here])
 
     def contract_incoming():
         for dy in columns:
@@ -260,7 +260,7 @@
                 for r in range(nr):
                     for half in range(2):
                         prod[1, half, r * nc + c0 + c] = part[r, half]
-            put_back(1, 0, [s for s in shifts + [here] if s[1] == dy])
+        put_back(1, 0, shifts + [here])
         put_back(1, 1, shifts + [here])
 
     def widen(u, half):
@@ -318,6 +318,10 @@
 
         for_each(B // q, left_next)
         pack(send_left.at[half], B)
+        if half == 0:
+            sent(send.at[0], send_sem.at[0])
+        else:
+            sent(send_left.at[0], left_send_sem.at[0])
         put_left(half)
     for copy in loads[6:]:
         copy.wait()
@@ -382,10 +386,10 @@
             copy = pltpu.make_async_copy(out_ref.at[rows], out_hbm.at[rows], out_sem.at[half * 2 + i])
             copy.start()
             outs.append(copy)
-    for i in range(3):
+    for i in (1, 2):
         sent(send.at[i], send_sem.at[i])
-    for half in range(2):
-        sent(send_left.at[half], left_send_sem.at[half])
+    sent(send_left.at[1], left_send_sem.at[1])
+    for half in range(2):
         for u in range(2):
             sent(prod.at[u, half], back_send_sem.at[u, half])
     for copy in outs:

time: 64.3 us -> 61.3 us (0.953)
  Pallas kernels: 62.2 us -> 59.3 us
    pallas_call x1, Pallas kernels: 62.2 us -> 59.3 us  [local(): pl.pallas_call(functools.partial(kernel, nr, nc), out_shape=jax.ShapeDtyp...]
where the time goes in v5:
time: 61.3 us; the launch traced here: 61.2 us
  Pallas kernels  59.3 us (97%)
  local copies, waits for them, and re-layouts  1.87 us (3%)
    pallas_call x1, Pallas kernels, local(): pl.pallas_call(functools.partial(kernel, nr, nc), out_shape=jax.ShapeDtyp...  59.3 us
    unnamed x1, local copies, waits for them, and re-layouts  1.87 us

profile of v5, /device:TPU:1, one launch (start us, length us, event | category | flops | bytes accessed | tf_op | source)
XLA Modules:
  0.0 61.2 jit_solution(7480641759432882132)
XLA Ops:
  0.0 59.3 %shard_map.82 = bf16[32,64,128]{2,1,0:T(8,128)(2,1)} custom-call(bf16[32,64,128]{2,1,0:T(8,128)(2,1)} %pair_hbm.1, s32[4,128]{1,0:T(4,128)} %bitcast.2, s32[4,128]{1,0:T(4,128)} %bitcast.3, bf16[2,128,512]{2,1,0:T(8,128)(2,1)} %w_in_hbm.1, bf16[2,128,128]{2,1,0:T(8,128)(2,1)} %w_gate_hbm.1, bf16[2,128,128]{2,1,0:T(8,128)(2,1)} %w_out_hbm.1, ...), custom_call_target="tpu_custom_call" | custom-call | tf_op jit(solution)/shard_map/pallas_call | solution.py:410
  59.3 1.9 %copy.10 = bf16[32,64,128]{2,1,0:T(8,128)(2,1)} copy(bf16[32,64,128]{2,1,0:T(8,128)(2,1)} %shard_map.82) | data formatting | bytes 1048576

commit v6 on v5

--- a/solution.py
+++ b/solution.py
@@ -319,17 +319,17 @@
         for_each(B // q, left_next)
         pack(send_left.at[half], B)
         if half == 0:
+            for copy in loads[6:]:
+                copy.wait()
+            turn_small(0)
+            gates(0)
             sent(send.at[0], send_sem.at[0])
         else:
+            turn_weights(1)
+            turn_small(1)
             sent(send_left.at[0], left_send_sem.at[0])
         put_left(half)
-    for copy in loads[6:]:
-        copy.wait()
     valid_cols = col_flags(valid_v)
-    turn_small(0)
-    gates(0)
-    turn_weights(1)
-    turn_small(1)
     factors = column(gain_ref, 0, 1, H), column(shift_ref, 0, 1, H)
     gain1, shift1 = column(gain_ref, 1, 0, C), column(shift_ref, 1, 0, C)
     arrive(got.at[0], got_sem.at[0])
@@ -435,9 +435,9 @@
                 dma((10,)), dma((3,)), dma((3,)), dma((2,)), dma((2,)), dma((2, 2)), dma((2, 2)), dma((4,)),
             ],
             compiler_params=pltpu.CompilerParams(
-                collective_id=0, has_side_effects=True, vmem_limit_bytes=60 * 1024 * 1024
+                collective_id=0, has_side_effects=True, vmem_limit_bytes=48 * 1024 * 1024
             ),
-        )(*operands)
+        )(*[pltpu.with_memory_space_constraint(a, pltpu.HBM) for a in operands])
 
     placed = (P("row", "col", None), P(), P(), P(), P(), P(), P(), P())
     return jax.shard_map(

time: 61.3 us -> 59.9 us (0.977)
  local copies, waits for them, and re-layouts: 1.87 us -> 0.8 us
    unnamed x1, local copies, waits for them, and re-layouts: 1.87 us -> 0.8 us
where the time goes in v6:
time: 59.9 us; the launch traced here: 59.8 us
  Pallas kernels  59 us (98%)
  local copies, waits for them, and re-layouts  0.8 us (1%)
    pallas_call x1, Pallas kernels, local(): pl.pallas_call(functools.partial(kernel, nr, nc), out_shape=jax.ShapeDtyp...  59 us

profile of v6, /device:TPU:1, one launch (start us, length us, event | category | flops | bytes accessed | tf_op | source)
XLA Modules:
  0.0 59.8 jit_solution(5157410436614572548)
XLA Ops:
  0.0 59.0 %shard_map.82 = bf16[32,64,128]{2,1,0:T(8,128)(2,1)S(1)} custom-call(bf16[32,64,128]{2,1,0:T(8,128)(2,1)} %pair_hbm.1, s32[4,128]{1,0:T(4,128)} %bitcast.2, s32[4,128]{1,0:T(4,128)} %bitcast.3, bf16[2,128,512]{2,1,0:T(8,128)(2,1)} %w_in_hbm.1, bf16[2,128,128]{2,1,0:T(8,128)(2,1)} %w_gate_hbm.1, bf16[2,128,128]{2,1,0:T(8,128)(2,1)} %w_out_hbm.1, ...), custom_call_target="tpu_custom_call" | custom-call | tf_op jit(solution)/shard_map/pallas_call | solution.py:410
  59.0 0.8 %copy.10 = bf16[32,64,128]{2,1,0:T(8,128)(2,1)} copy(bf16[32,64,128]{2,1,0:T(8,128)(2,1)S(1)} %shard_map.82) | data formatting | bytes 1048576

commit v7 on v6

--- a/solution.py
+++ b/solution.py
@@ -142,7 +142,7 @@
 
     def for_each(n, step):
         if n:
-            lax.fori_loop(0, n, step, 0)
+            lax.fori_loop(0, n, step, 0, unroll=n <= 2)
 
     def gates(u):
         def chunk(g, carry):

time: 59.9 us -> 59.4 us (level)
  no operation moved by 1% of the time
where the time goes in v7:
time: 59.4 us; the launch traced here: 59.3 us
  Pallas kernels  58.5 us (98%)
  local copies, waits for them, and re-layouts  0.8 us (1%)
    pallas_call x1, Pallas kernels, local(): pl.pallas_call(functools.partial(kernel, nr, nc), out_shape=jax.ShapeDtyp...  58.5 us

profile of v7, /device:TPU:1, one launch (start us, length us, event | category | flops | bytes accessed | tf_op | source)
XLA Modules:
  0.0 59.3 jit_solution(3337762687464192629)
XLA Ops:
  0.0 58.5 %shard_map.82 = bf16[32,64,128]{2,1,0:T(8,128)(2,1)S(1)} custom-call(bf16[32,64,128]{2,1,0:T(8,128)(2,1)} %pair_hbm.1, s32[4,128]{1,0:T(4,128)} %bitcast.2, s32[4,128]{1,0:T(4,128)} %bitcast.3, bf16[2,128,512]{2,1,0:T(8,128)(2,1)} %w_in_hbm.1, bf16[2,128,128]{2,1,0:T(8,128)(2,1)} %w_gate_hbm.1, bf16[2,128,128]{2,1,0:T(8,128)(2,1)} %w_out_hbm.1, ...), custom_call_target="tpu_custom_call" | custom-call | tf_op jit(solution)/shard_map/pallas_call | solution.py:410
  58.5 0.8 %copy.10 = bf16[32,64,128]{2,1,0:T(8,128)(2,1)} copy(bf16[32,64,128]{2,1,0:T(8,128)(2,1)S(1)} %shard_map.82) | data formatting | bytes 1048576

commit v8 on v7

--- a/solution.py
+++ b/solution.py
@@ -125,7 +125,9 @@
         return (centred * lax.rsqrt(variance + EPS) * gain + shift).astype(BF16)
 
     def project(u, side, normed, mask, at, stride):
-        both = dot(wt[u, side * 2 * H:(side + 1) * 2 * H, :], normed)
+        place(dot(wt[u, side * 2 * H:(side + 1) * 2 * H, :], normed), mask, at, stride)
+
+    def place(both, mask, at, stride):
         value = both[:H] * (sigmoid(both[H:]) * mask)
         for t in range(q):
             lay[pl.ds(at + t, H, stride=stride), :] = value[:, t * 128:(t + 1) * 128]
@@ -353,8 +355,9 @@
             normed = jnp.concatenate(normed, axis=1)
             nb[half * (B // q) + g] = normed
             mask = flags(pad_s, pad_cols, i2)
-            project(1, 1, normed, mask, g * q, T)
-            project(1, 0, normed, mask, B + g * q, T)
+            every = dot(wt[1], normed)
+            place(every[2 * H:], mask, g * q, T)
+            place(every[:2 * H], mask, B + g * q, T)
             return carry
 
         for_each(B // q, middle)

time: 59.4 us -> 59.4 us (level)
  no operation moved by 1% of the time
where the time goes in v8:
time: 59.4 us; the launch traced here: 59.3 us
  Pallas kernels  58.5 us (98%)
  local copies, waits for them, and re-layouts  0.8 us (1%)
    pallas_call x1, Pallas kernels, local(): pl.pallas_call(functools.partial(kernel, nr, nc), out_shape=jax.ShapeDtyp...  58.5 us

profile of v8, /device:TPU:1, one launch (start us, length us, event | category | flops | bytes accessed | tf_op | source)
XLA Modules:
  0.0 59.3 jit_solution(11538029069875669871)
XLA Ops:
  0.0 58.5 %shard_map.82 = bf16[32,64,128]{2,1,0:T(8,128)(2,1)S(1)} custom-call(bf16[32,64,128]{2,1,0:T(8,128)(2,1)} %pair_hbm.1, s32[4,128]{1,0:T(4,128)} %bitcast.2, s32[4,128]{1,0:T(4,128)} %bitcast.3, bf16[2,128,512]{2,1,0:T(8,128)(2,1)} %w_in_hbm.1, bf16[2,128,128]{2,1,0:T(8,128)(2,1)} %w_gate_hbm.1, bf16[2,128,128]{2,1,0:T(8,128)(2,1)} %w_out_hbm.1, ...), custom_call_target="tpu_custom_call" | custom-call | tf_op jit(solution)/shard_map/pallas_call | solution.py:413
  58.6 0.8 %copy.10 = bf16[32,64,128]{2,1,0:T(8,128)(2,1)} copy(bf16[32,64,128]{2,1,0:T(8,128)(2,1)S(1)} %shard_map.82) | data formatting | bytes 1048576
